TPU v7x, 768 devices: a whole 4x8x12 slice. The times are simulated.
768 devices in a mesh: lon: 24 (over z, y_hi), lat: 32 (over x, y_lo, core).
Axes of the slice: x: 4, y: 8 (y_hi: 2, y_lo: 4; y = y_hi * 4 + y_lo), z: 12, core: 2. Of those that a mesh axis runs over, the one named last changes fastest.
Arguments:
- tracers: float32 [3, 8, 256, 3072], P(None, None, 'lat', 'lon'), may hold values from -6 to 6
- cotangent: float32 [3, 8, 256, 3072], P(None, None, 'lat', 'lon'), may hold values from -6 to 6
- east_vel: float32 [8, 256, 3072], P(None, 'lat', 'lon'), may hold values from -0.3 to 0.3
- north_vel: float32 [8, 256, 3072], P(None, 'lat', 'lon'), may hold values from -0.3 to 0.3
- sea_mask: int32 [256, 3072], P('lat', 'lon'), may hold values 0 or 1
- level_count: int32 [256, 3072], P('lat', 'lon'), may hold values from 1 to 8
Outputs:
- adj_tracers: float32 [3, 8, 256, 3072], P(None, None, 'lat', 'lon')
- adj_east: float32 [8, 256, 3072], P(None, 'lat', 'lon')
- adj_north: float32 [8, 256, 3072], P(None, 'lat', 'lon')
All inputs are finite; a program needn't handle non-finite values. No bound on the sum of `sea_mask` on one device may be relied on, other than what follows from the above.
Results may differ from a plain program's by a relative error of at most 0.00002.
Values sent between devices are 32-bit elements; how exact they have to be, the bound alone decides.
A program may use at most 32 MiB of HBM per device.

v0:
```python
import jax
import jax.numpy as jnp
from jax import lax
from jax.sharding import PartitionSpec as P

STEPS = 4


horiz_diff = 0.22
vert_diff = 0.05


def extended_2(cells, sides, width, closed):
    for axis, dim in sides:
        count = lax.axis_size(axis)
        ends = count if closed else count - 1
        head = lax.slice_in_dim(cells, 0, width, axis=dim)
        tail = lax.slice_in_dim(cells, cells.shape[dim] - width, cells.shape[dim], axis=dim)
        cells = jnp.concatenate(
            [
                lax.ppermute(tail, axis, [(i, (i + 1) % count) for i in range(ends)]),
                cells,
                lax.ppermute(head, axis, [((i + 1) % count, i) for i in range(ends)]),
            ],
            axis=dim,
        )
    return cells


def advance(tracer, east_field, north_field, wetness):
    row_part = tracer[..., 1:-1, :]
    row_wet = wetness[:, 1:-1, :]
    east_open = row_wet[:, :, :-1] * row_wet[:, :, 1:]
    east_flux = east_open * (
        east_field[:, 1:-1, :-1] * 0.5 * (row_part[..., :-1] + row_part[..., 1:])
        - horiz_diff * (row_part[..., 1:] - row_part[..., :-1])
    )
    column_part = tracer[..., :, 1:-1]
    column_wet = wetness[:, :, 1:-1]
    north_open = column_wet[:, :-1, :] * column_wet[:, 1:, :]
    north_flux = north_open * (
        north_field[:, :-1, 1:-1] * 0.5 * (column_part[..., :-1, :] + column_part[..., 1:, :])
        - horiz_diff * (column_part[..., 1:, :] - column_part[..., :-1, :])
    )
    centre = tracer[..., 1:-1, 1:-1]
    centre_wet = wetness[:, 1:-1, 1:-1]
    vertical_open = centre_wet[:-1] * centre_wet[1:]
    vertical_flux = vertical_open * vert_diff * (centre[..., 1:, :, :] - centre[..., :-1, :, :])
    nothing = jnp.zeros_like(centre[..., :1, :, :])
    mixing = jnp.concatenate([vertical_flux, nothing], -3) - jnp.concatenate(
        [nothing, vertical_flux], -3
    )
    return centre_wet * (
        centre
        - (east_flux[..., 1:] - east_flux[..., :-1])
        - (north_flux[..., 1:, :] - north_flux[..., :-1, :])
        + mixing
    )


def clear_outside(extended, rim_width):
    lat_place = lax.axis_index("lat")
    lat_total = lax.axis_size("lat")
    row_index = lax.broadcasted_iota(jnp.int32, extended.shape, 1)
    keep_cell = ((row_index >= rim_width) | (lat_place > 0)) & (
        (row_index < extended.shape[1] - rim_width) | (lat_place < lat_total - 1)
    )
    return jnp.where(keep_cell, extended, jnp.zeros_like(extended))


def extend_state(field_in, rim_width):
    extended = extended_2(field_in, (("lon", 2), ("lat", 1)), rim_width, True)
    return clear_outside(extended, rim_width)


def extend_static(field_in, rim_width):
    extended = extended_2(field_in, (("lon", 2), ("lat", 1)), rim_width, True)
    return clear_outside(extended, rim_width)


def return_rims(gradient, rim_width):
    lon_cols = gradient.shape[2] - 2 * rim_width
    lat_rows = gradient.shape[1] - 2 * rim_width
    margins = jnp.concatenate([gradient[..., :rim_width], gradient[..., lon_cols + rim_width :]], 2)
    arrived = extended_2(margins, (("lon", 2),), rim_width, True)
    inner_part = gradient[..., rim_width : lon_cols + rim_width]
    inner_part = inner_part.at[..., :rim_width].add(arrived[..., :rim_width])
    inner_part = inner_part.at[..., lon_cols - rim_width :].add(arrived[..., 3 * rim_width :])
    margins = jnp.concatenate([inner_part[:, :rim_width], inner_part[:, lat_rows + rim_width :]], 1)
    arrived = extended_2(margins, (("lat", 1),), rim_width, False)
    result = inner_part[:, rim_width : lat_rows + rim_width]
    result = result.at[:, :rim_width].add(arrived[:, :rim_width])
    return result.at[:, lat_rows - rim_width :].add(arrived[:, 3 * rim_width :])


def on_device(tracers, cotangent, east_vel, north_vel, sea_mask, level_count):
    tracer_count = tracers.shape[0]
    level_total = east_vel.shape[0]
    lat_rows = east_vel.shape[1]
    lon_cols = east_vel.shape[2]
    stacked_count = tracer_count * level_total
    level_index = lax.broadcasted_iota(jnp.int32, east_vel.shape, 0)
    wet_field = jnp.where(
        (sea_mask[None] == 1) & (level_index < level_count[None]), 1.0, 0.0
    ).astype(jnp.float32)
    static_fields = jnp.concatenate([east_vel, north_vel, wet_field], 0)
    state_flat = (stacked_count, lat_rows, lon_cols)
    static_wide = extend_static(static_fields, 1)
    east_wide = static_wide[:level_total]
    north_wide = static_wide[level_total : 2 * level_total]
    wet_wide = static_wide[2 * level_total :]

    def local_step(widened, east_field, north_field):
        return advance(widened, east_field, north_field, wet_wide)

    current = tracers
    stored = []
    for repeat in range(STEPS):
        widened = extend_state(current.reshape(state_flat), 1).reshape(
            tracer_count, level_total, lat_rows + 2, lon_cols + 2
        )
        stored.append(widened)
        current = local_step(widened, east_wide, north_wide)
    adjoint = cotangent
    east_total = jnp.zeros_like(east_wide)
    north_total = jnp.zeros_like(north_wide)
    for repeat in reversed(range(STEPS)):
        ignored, pullback = jax.vjp(local_step, stored[repeat], east_wide, north_wide)
        back_state, back_east, back_north = pullback(adjoint)
        east_total = east_total + back_east
        north_total = north_total + back_north
        flat_state = back_state.reshape((stacked_count,) + back_state.shape[2:])
        if repeat > 0:
            adjoint = return_rims(flat_state, 1).reshape(tracers.shape)
        else:
            returned = return_rims(jnp.concatenate([flat_state, east_total, north_total], 0), 1)
    adjoint = returned[:stacked_count].reshape(tracers.shape)
    return (
        adjoint,
        returned[stacked_count : stacked_count + level_total],
        returned[stacked_count + level_total :],
    )


def solution(mesh):
    placed = (
        P(None, None, "lat", "lon"),
        P(None, None, "lat", "lon"),
        P(None, "lat", "lon"),
        P(None, "lat", "lon"),
        P("lat", "lon"),
        P("lat", "lon"),
    )
    return jax.shard_map(
        on_device,
        mesh=mesh,
        in_specs=placed,
        out_specs=(P(None, None, "lat", "lon"), P(None, "lat", "lon"), P(None, "lat", "lon")),
        check_vma=False,
    )
```

profile of v0, /device:TPU:59, one launch (start us, length us, event | category | flops | bytes accessed | tf_op | source)
XLA Modules:
  0.0 300.7 jit_solution(4181588431383237597)
XLA Ops:
  2.3 6.2 %collective-permute-start = (f32[24,8,1]{2,1,0:T(8,128)S(1)}, f32[24,8,1]{2,1,0:T(8,128)S(1)}, u32[]{:S(2)}, u32[]{:S(2)}) collective-permute-start(f32[24,8,1]{2,1,0:T(8,128)S(1)} %get-tuple-element.287), channel_id=1, source_target_pairs={{0,32},{32,64},{64,96},{96,128},{128,160},{160,192},{192,224},{224... | collective-permute-start | bytes 2312 | tf_op jit(solution)/shard_map/ppermute | solution.py:21
  11.6 7.1 %collective-permute-start.16 = (f32[24,8,1]{2,1,0:T(8,128)S(1)}, f32[24,8,1]{2,1,0:T(8,128)S(1)}, u32[]{:S(2)}, u32[]{:S(2)}) collective-permute-start(f32[24,8,1]{2,1,0:T(8,128)S(1)} %get-tuple-element.289), channel_id=1, source_target_pairs={{0,32},{32,64},{64,96},{96,128},{128,160},{160,192},{192,224},{224... | collective-permute-start | bytes 2312 | tf_op jit(solution)/shard_map/ppermute | solution.py:21
  18.7 8.8 %collective-permute-start.17 = (f32[24,8,1]{2,1,0:T(8,128)S(1)}, f32[24,8,1]{2,1,0:T(8,128)S(1)}, u32[]{:S(2)}, u32[]{:S(2)}) collective-permute-start(f32[24,8,1]{2,1,0:T(8,128)S(1)} %get-tuple-element.290), channel_id=1, source_target_pairs={{32,0},{64,32},{96,64},{128,96},{160,128},{192,160},{224,192},{256... | collective-permute-start | bytes 2312 | tf_op jit(solution)/shard_map/ppermute | solution.py:23
  27.8 6.6 %collective-permute-start.2 = (f32[24,1,130]{2,1,0:T(1,128)S(1)}, f32[24,1,130]{2,1,0:T(1,128)S(1)}, u32[]{:S(2)}, u32[]{:S(2)}) collective-permute-start(f32[24,1,130]{2,1,0:T(1,128)S(1)} %get-tuple-element.255), channel_id=1, source_target_pairs={{0,1},{1,2},{2,3},{3,4},{4,5},{5,6},{6,7},{7,8},{8,9},{9,10},{10,1... | collective-permute-start | bytes 37448 | tf_op jit(solution)/shard_map/ppermute | solution.py:21
  39.0 5.8 %collective-permute-start.18 = (f32[24,1,130]{2,1,0:T(1,128)S(1)}, f32[24,1,130]{2,1,0:T(1,128)S(1)}, u32[]{:S(2)}, u32[]{:S(2)}) collective-permute-start(f32[24,1,130]{2,1,0:T(1,128)S(1)} %get-tuple-element.257), channel_id=1, source_target_pairs={{0,1},{1,2},{2,3},{3,4},{4,5},{5,6},{6,7},{7,8},{8,9},{9,10},{10,1... | collective-permute-start | bytes 37448 | tf_op jit(solution)/shard_map/ppermute | solution.py:21
  49.8 9.7 %collective-permute-start.5 = (f32[24,10,1]{2,1,0:T(8,128)S(1)}, f32[24,10,1]{2,1,0:T(8,128)S(1)}, u32[]{:S(2)}, u32[]{:S(2)}) collective-permute-start(f32[24,10,1]{2,1,0:T(8,128)S(1)} %get-tuple-element.241), channel_id=1, source_target_pairs={{32,0},{64,32},{96,64},{128,96},{160,128},{192,160},{224,192},{256... | collective-permute-start | bytes 2888 | tf_op jit(solution)/shard_map/ppermute | solution.py:23
  59.5 13.7 %collective-permute-done.4 = f32[24,10,1]{2,1,0:T(8,128)S(1)} collective-permute-done((f32[24,10,1]{2,1,0:T(8,128)S(1)}, f32[24,10,1]{2,1,0:T(8,128)S(1)}, u32[]{:S(2)}, u32[]{:S(2)}) %collective-permute-start.4) | collective-permute-done | bytes 992 | tf_op jit(solution)/shard_map/ppermute | solution.py:21
  82.7 5.7 %collective-permute-done.7 = f32[24,1,128]{2,1,0:T(1,128)S(1)} collective-permute-done((f32[24,1,128]{2,1,0:T(1,128)S(1)}, f32[24,1,128]{2,1,0:T(1,128)S(1)}, u32[]{:S(2)}, u32[]{:S(2)}) %collective-permute-start.7) | collective-permute-done | bytes 12320 | tf_op jit(solution)/shard_map/ppermute | solution.py:23
  90.6 7.3 %collective-permute-start.21 = (f32[24,8,1]{2,1,0:T(8,128)S(1)}, f32[24,8,1]{2,1,0:T(8,128)S(1)}, u32[]{:S(2)}, u32[]{:S(2)}) collective-permute-start(f32[24,8,1]{2,1,0:T(8,128)S(1)} %get-tuple-element.286), channel_id=1, source_target_pairs={{32,0},{64,32},{96,64},{128,96},{160,128},{192,160},{224,192},{256... | collective-permute-start | bytes 2312 | tf_op jit(solution)/shard_map/ppermute | solution.py:23
  107.0 5.9 %collective-permute-done.23 = f32[24,1,130]{2,1,0:T(1,128)S(1)} collective-permute-done((f32[24,1,130]{2,1,0:T(1,128)S(1)}, f32[24,1,130]{2,1,0:T(1,128)S(1)}, u32[]{:S(2)}, u32[]{:S(2)}) %collective-permute-start.23) | collective-permute-done | bytes 12512 | tf_op jit(solution)/shard_map/ppermute | solution.py:23
  116.4 7.3 %collective-permute-start.9 = (f32[24,10,1]{2,1,0:T(8,128)S(1)}, f32[24,10,1]{2,1,0:T(8,128)S(1)}, u32[]{:S(2)}, u32[]{:S(2)}) collective-permute-start(f32[24,10,1]{2,1,0:T(8,128)S(1)} %get-tuple-element.239), channel_id=1, source_target_pairs={{32,0},{64,32},{96,64},{128,96},{160,128},{192,160},{224,192},{256... | collective-permute-start | bytes 2888 | tf_op jit(solution)/shard_map/ppermute | solution.py:23
  123.7 9.9 %collective-permute-done.8 = f32[24,10,1]{2,1,0:T(8,128)S(1)} collective-permute-done((f32[24,10,1]{2,1,0:T(8,128)S(1)}, f32[24,10,1]{2,1,0:T(8,128)S(1)}, u32[]{:S(2)}, u32[]{:S(2)}) %collective-permute-start.8) | collective-permute-done | bytes 992 | tf_op jit(solution)/shard_map/ppermute | solution.py:21
  145.5 5.7 %collective-permute-done.11 = f32[24,1,128]{2,1,0:T(1,128)S(1)} collective-permute-done((f32[24,1,128]{2,1,0:T(1,128)S(1)}, f32[24,1,128]{2,1,0:T(1,128)S(1)}, u32[]{:S(2)}, u32[]{:S(2)}) %collective-permute-start.11) | collective-permute-done | bytes 12320 | tf_op jit(solution)/shard_map/ppermute | solution.py:23
  153.4 7.3 %collective-permute-start.25 = (f32[24,8,1]{2,1,0:T(8,128)S(1)}, f32[24,8,1]{2,1,0:T(8,128)S(1)}, u32[]{:S(2)}, u32[]{:S(2)}) collective-permute-start(f32[24,8,1]{2,1,0:T(8,128)S(1)} %get-tuple-element.284), channel_id=1, source_target_pairs={{32,0},{64,32},{96,64},{128,96},{160,128},{192,160},{224,192},{256... | collective-permute-start | bytes 2312 | tf_op jit(solution)/shard_map/ppermute | solution.py:23
  170.6 5.9 %collective-permute-done.27 = f32[24,1,130]{2,1,0:T(1,128)S(1)} collective-permute-done((f32[24,1,130]{2,1,0:T(1,128)S(1)}, f32[24,1,130]{2,1,0:T(1,128)S(1)}, u32[]{:S(2)}, u32[]{:S(2)}) %collective-permute-start.27) | collective-permute-done | bytes 12512 | tf_op jit(solution)/shard_map/ppermute | solution.py:23
  180.0 8.1 %collective-permute-start.13 = (f32[24,10,1]{2,1,0:T(8,128)S(1)}, f32[24,10,1]{2,1,0:T(8,128)S(1)}, u32[]{:S(2)}, u32[]{:S(2)}) collective-permute-start(f32[24,10,1]{2,1,0:T(8,128)S(1)} %get-tuple-element.237), channel_id=1, source_target_pairs={{32,0},{64,32},{96,64},{128,96},{160,128},{192,160},{224,192},{256... | collective-permute-start | bytes 2888 | tf_op jit(solution)/shard_map/ppermute | solution.py:23
  188.1 9.5 %collective-permute-done.12 = f32[24,10,1]{2,1,0:T(8,128)S(1)} collective-permute-done((f32[24,10,1]{2,1,0:T(8,128)S(1)}, f32[24,10,1]{2,1,0:T(8,128)S(1)}, u32[]{:S(2)}, u32[]{:S(2)}) %collective-permute-start.12) | collective-permute-done | bytes 992 | tf_op jit(solution)/shard_map/ppermute | solution.py:21
  209.5 5.7 %collective-permute-done.15 = f32[24,1,128]{2,1,0:T(1,128)S(1)} collective-permute-done((f32[24,1,128]{2,1,0:T(1,128)S(1)}, f32[24,1,128]{2,1,0:T(1,128)S(1)}, u32[]{:S(2)}, u32[]{:S(2)}) %collective-permute-start.15) | collective-permute-done | bytes 12320 | tf_op jit(solution)/shard_map/ppermute | solution.py:23
  217.6 7.9 %collective-permute-start.29 = (f32[24,8,1]{2,1,0:T(8,128)S(1)}, f32[24,8,1]{2,1,0:T(8,128)S(1)}, u32[]{:S(2)}, u32[]{:S(2)}) collective-permute-start(f32[24,8,1]{2,1,0:T(8,128)S(1)} %get-tuple-element.282), channel_id=1, source_target_pairs={{32,0},{64,32},{96,64},{128,96},{160,128},{192,160},{224,192},{256... | collective-permute-start | bytes 2312 | tf_op jit(solution)/shard_map/ppermute | solution.py:23
  235.3 5.6 %collective-permute-done.31 = f32[24,1,130]{2,1,0:T(1,128)S(1)} collective-permute-done((f32[24,1,130]{2,1,0:T(1,128)S(1)}, f32[24,1,130]{2,1,0:T(1,128)S(1)}, u32[]{:S(2)}, u32[]{:S(2)}) %collective-permute-start.31) | collective-permute-done | bytes 12512 | tf_op jit(solution)/shard_map/ppermute | solution.py:23
  244.9 8.1 %collective-permute-start.33 = (f32[40,10,1]{2,1,0:T(8,128)S(1)}, f32[40,10,1]{2,1,0:T(8,128)S(1)}, u32[]{:S(2)}, u32[]{:S(2)}) collective-permute-start(f32[40,10,1]{2,1,0:T(8,128)S(1)} %get-tuple-element.235), channel_id=1, source_target_pairs={{32,0},{64,32},{96,64},{128,96},{160,128},{192,160},{224,192},{256... | collective-permute-start | bytes 4808 | tf_op jit(solution)/shard_map/ppermute | solution.py:23
  252.9 22.8 %collective-permute-done.32 = f32[40,10,1]{2,1,0:T(8,128)S(1)} collective-permute-done((f32[40,10,1]{2,1,0:T(8,128)S(1)}, f32[40,10,1]{2,1,0:T(8,128)S(1)}, u32[]{:S(2)}, u32[]{:S(2)}) %collective-permute-start.32) | collective-permute-done | bytes 1632 | tf_op jit(solution)/shard_map/ppermute | solution.py:21
  284.2 7.2 %collective-permute-start.34 = (f32[40,1,128]{2,1,0:T(1,128)S(1)}, f32[40,1,128]{2,1,0:T(1,128)S(1)}, u32[]{:S(2)}, u32[]{:S(2)}) collective-permute-start(f32[40,1,128]{2,1,0:T(1,128)S(1)} %get-tuple-element.248), channel_id=1, source_target_pairs={{0,1},{1,2},{2,3},{3,4},{4,5},{5,6},{6,7},{7,8},{8,9},{9,10},{10,1... | collective-permute-start | bytes 61448 | tf_op jit(solution)/shard_map/ppermute | solution.py:21
  293.5 5.7 %collective-permute-done.35 = f32[40,1,128]{2,1,0:T(1,128)S(1)} collective-permute-done((f32[40,1,128]{2,1,0:T(1,128)S(1)}, f32[40,1,128]{2,1,0:T(1,128)S(1)}, u32[]{:S(2)}, u32[]{:S(2)}) %collective-permute-start.35) | collective-permute-done | bytes 20512 | tf_op jit(solution)/shard_map/ppermute | solution.py:23
  (172 shorter events, 105.4 us)
Async XLA Ops:
  2.3 25.3 %collective-permute-start = (f32[24,8,1]{2,1,0:T(8,128)S(1)}, f32[24,8,1]{2,1,0:T(8,128)S(1)}, u32[]{:S(2)}, u32[]{:S(2)}) collective-permute-start(f32[24,8,1]{2,1,0:T(8,128)S(1)} %get-tuple-element.287), channel_id=1, source_target_pairs={{0,32},{32,64},{64,96},{96,128},{128,160},{160,192},{192,224},{224... | collective-permute-start | bytes 2312 | tf_op jit(solution)/shard_map/ppermute | solution.py:21
  8.5 19.1 %collective-permute-start.1 = (f32[24,8,1]{2,1,0:T(8,128)S(1)}, f32[24,8,1]{2,1,0:T(8,128)S(1)}, u32[]{:S(2)}, u32[]{:S(2)}) collective-permute-start(f32[24,8,1]{2,1,0:T(8,128)S(1)} %get-tuple-element.288), channel_id=1, source_target_pairs={{32,0},{64,32},{96,64},{128,96},{160,128},{192,160},{224,192},{256... | collective-permute-start | bytes 2312 | tf_op jit(solution)/shard_map/ppermute | solution.py:23
  11.6 24.8 %collective-permute-start.16 = (f32[24,8,1]{2,1,0:T(8,128)S(1)}, f32[24,8,1]{2,1,0:T(8,128)S(1)}, u32[]{:S(2)}, u32[]{:S(2)}) collective-permute-start(f32[24,8,1]{2,1,0:T(8,128)S(1)} %get-tuple-element.289), channel_id=1, source_target_pairs={{0,32},{32,64},{64,96},{96,128},{128,160},{160,192},{192,224},{224... | collective-permute-start | bytes 2312 | tf_op jit(solution)/shard_map/ppermute | solution.py:21
  18.7 17.6 %collective-permute-start.17 = (f32[24,8,1]{2,1,0:T(8,128)S(1)}, f32[24,8,1]{2,1,0:T(8,128)S(1)}, u32[]{:S(2)}, u32[]{:S(2)}) collective-permute-start(f32[24,8,1]{2,1,0:T(8,128)S(1)} %get-tuple-element.290), channel_id=1, source_target_pairs={{32,0},{64,32},{96,64},{128,96},{160,128},{192,160},{224,192},{256... | collective-permute-start | bytes 2312 | tf_op jit(solution)/shard_map/ppermute | solution.py:23
  27.8 17.1 %collective-permute-start.2 = (f32[24,1,130]{2,1,0:T(1,128)S(1)}, f32[24,1,130]{2,1,0:T(1,128)S(1)}, u32[]{:S(2)}, u32[]{:S(2)}) collective-permute-start(f32[24,1,130]{2,1,0:T(1,128)S(1)} %get-tuple-element.255), channel_id=1, source_target_pairs={{0,1},{1,2},{2,3},{3,4},{4,5},{5,6},{6,7},{7,8},{8,9},{9,10},{10,1... | collective-permute-start | bytes 37448 | tf_op jit(solution)/shard_map/ppermute | solution.py:21
  34.4 10.5 %collective-permute-start.3 = (f32[24,1,130]{2,1,0:T(1,128)S(1)}, f32[24,1,130]{2,1,0:T(1,128)S(1)}, u32[]{:S(2)}, u32[]{:S(2)}) collective-permute-start(f32[24,1,130]{2,1,0:T(1,128)S(1)} %get-tuple-element.256), channel_id=1, source_target_pairs={{1,0},{2,1},{3,2},{4,3},{5,4},{6,5},{7,6},{8,7},{9,8},{10,9},{11,1... | collective-permute-start | bytes 37448 | tf_op jit(solution)/shard_map/ppermute | solution.py:23
  36.6 9.7 %collective-permute-start.19 = (f32[24,1,130]{2,1,0:T(1,128)S(1)}, f32[24,1,130]{2,1,0:T(1,128)S(1)}, u32[]{:S(2)}, u32[]{:S(2)}) collective-permute-start(f32[24,1,130]{2,1,0:T(1,128)S(1)} %get-tuple-element.258), channel_id=1, source_target_pairs={{1,0},{2,1},{3,2},{4,3},{5,4},{6,5},{7,6},{8,7},{9,8},{10,9},{11,1... | collective-permute-start | bytes 37448 | tf_op jit(solution)/shard_map/ppermute | solution.py:23
  47.8 25.4 %collective-permute-start.4 = (f32[24,10,1]{2,1,0:T(8,128)S(1)}, f32[24,10,1]{2,1,0:T(8,128)S(1)}, u32[]{:S(2)}, u32[]{:S(2)}) collective-permute-start(f32[24,10,1]{2,1,0:T(8,128)S(1)} %get-tuple-element.242), channel_id=1, source_target_pairs={{0,32},{32,64},{64,96},{96,128},{128,160},{160,192},{192,224},{224... | collective-permute-start | bytes 2888 | tf_op jit(solution)/shard_map/ppermute | solution.py:21
  49.8 23.7 %collective-permute-start.5 = (f32[24,10,1]{2,1,0:T(8,128)S(1)}, f32[24,10,1]{2,1,0:T(8,128)S(1)}, u32[]{:S(2)}, u32[]{:S(2)}) collective-permute-start(f32[24,10,1]{2,1,0:T(8,128)S(1)} %get-tuple-element.241), channel_id=1, source_target_pairs={{32,0},{64,32},{96,64},{128,96},{160,128},{192,160},{224,192},{256... | collective-permute-start | bytes 2888 | tf_op jit(solution)/shard_map/ppermute | solution.py:23
  88.7 10.7 %collective-permute-start.20 = (f32[24,8,1]{2,1,0:T(8,128)S(1)}, f32[24,8,1]{2,1,0:T(8,128)S(1)}, u32[]{:S(2)}, u32[]{:S(2)}) collective-permute-start(f32[24,8,1]{2,1,0:T(8,128)S(1)} %get-tuple-element.285), channel_id=1, source_target_pairs={{0,32},{32,64},{64,96},{96,128},{128,160},{160,192},{192,224},{224... | collective-permute-start | bytes 2312 | tf_op jit(solution)/shard_map/ppermute | solution.py:21
  90.6 10.9 %collective-permute-start.21 = (f32[24,8,1]{2,1,0:T(8,128)S(1)}, f32[24,8,1]{2,1,0:T(8,128)S(1)}, u32[]{:S(2)}, u32[]{:S(2)}) collective-permute-start(f32[24,8,1]{2,1,0:T(8,128)S(1)} %get-tuple-element.286), channel_id=1, source_target_pairs={{32,0},{64,32},{96,64},{128,96},{160,128},{192,160},{224,192},{256... | collective-permute-start | bytes 2312 | tf_op jit(solution)/shard_map/ppermute | solution.py:23
  105.1 7.8 %collective-permute-start.23 = (f32[24,1,130]{2,1,0:T(1,128)S(1)}, f32[24,1,130]{2,1,0:T(1,128)S(1)}, u32[]{:S(2)}, u32[]{:S(2)}) collective-permute-start(f32[24,1,130]{2,1,0:T(1,128)S(1)} %get-tuple-element.254), channel_id=1, source_target_pairs={{1,0},{2,1},{3,2},{4,3},{5,4},{6,5},{7,6},{8,7},{9,8},{10,9},{11,1... | collective-permute-start | bytes 37448 | tf_op jit(solution)/shard_map/ppermute | solution.py:23
  114.3 19.2 %collective-permute-start.8 = (f32[24,10,1]{2,1,0:T(8,128)S(1)}, f32[24,10,1]{2,1,0:T(8,128)S(1)}, u32[]{:S(2)}, u32[]{:S(2)}) collective-permute-start(f32[24,10,1]{2,1,0:T(8,128)S(1)} %get-tuple-element.240), channel_id=1, source_target_pairs={{0,32},{32,64},{64,96},{96,128},{128,160},{160,192},{192,224},{224... | collective-permute-start | bytes 2888 | tf_op jit(solution)/shard_map/ppermute | solution.py:21
  116.4 20.5 %collective-permute-start.9 = (f32[24,10,1]{2,1,0:T(8,128)S(1)}, f32[24,10,1]{2,1,0:T(8,128)S(1)}, u32[]{:S(2)}, u32[]{:S(2)}) collective-permute-start(f32[24,10,1]{2,1,0:T(8,128)S(1)} %get-tuple-element.239), channel_id=1, source_target_pairs={{32,0},{64,32},{96,64},{128,96},{160,128},{192,160},{224,192},{256... | collective-permute-start | bytes 2888 | tf_op jit(solution)/shard_map/ppermute | solution.py:23
  151.5 9.8 %collective-permute-start.24 = (f32[24,8,1]{2,1,0:T(8,128)S(1)}, f32[24,8,1]{2,1,0:T(8,128)S(1)}, u32[]{:S(2)}, u32[]{:S(2)}) collective-permute-start(f32[24,8,1]{2,1,0:T(8,128)S(1)} %get-tuple-element.283), channel_id=1, source_target_pairs={{0,32},{32,64},{64,96},{96,128},{128,160},{160,192},{192,224},{224... | collective-permute-start | bytes 2312 | tf_op jit(solution)/shard_map/ppermute | solution.py:21
  153.4 11.0 %collective-permute-start.25 = (f32[24,8,1]{2,1,0:T(8,128)S(1)}, f32[24,8,1]{2,1,0:T(8,128)S(1)}, u32[]{:S(2)}, u32[]{:S(2)}) collective-permute-start(f32[24,8,1]{2,1,0:T(8,128)S(1)} %get-tuple-element.284), channel_id=1, source_target_pairs={{32,0},{64,32},{96,64},{128,96},{160,128},{192,160},{224,192},{256... | collective-permute-start | bytes 2312 | tf_op jit(solution)/shard_map/ppermute | solution.py:23
  168.7 7.8 %collective-permute-start.27 = (f32[24,1,130]{2,1,0:T(1,128)S(1)}, f32[24,1,130]{2,1,0:T(1,128)S(1)}, u32[]{:S(2)}, u32[]{:S(2)}) collective-permute-start(f32[24,1,130]{2,1,0:T(1,128)S(1)} %get-tuple-element.252), channel_id=1, source_target_pairs={{1,0},{2,1},{3,2},{4,3},{5,4},{6,5},{7,6},{8,7},{9,8},{10,9},{11,1... | collective-permute-start | bytes 37448 | tf_op jit(solution)/shard_map/ppermute | solution.py:23
  177.9 19.7 %collective-permute-start.12 = (f32[24,10,1]{2,1,0:T(8,128)S(1)}, f32[24,10,1]{2,1,0:T(8,128)S(1)}, u32[]{:S(2)}, u32[]{:S(2)}) collective-permute-start(f32[24,10,1]{2,1,0:T(8,128)S(1)} %get-tuple-element.238), channel_id=1, source_target_pairs={{0,32},{32,64},{64,96},{96,128},{128,160},{160,192},{192,224},{224... | collective-permute-start | bytes 2888 | tf_op jit(solution)/shard_map/ppermute | solution.py:21
  180.0 21.9 %collective-permute-start.13 = (f32[24,10,1]{2,1,0:T(8,128)S(1)}, f32[24,10,1]{2,1,0:T(8,128)S(1)}, u32[]{:S(2)}, u32[]{:S(2)}) collective-permute-start(f32[24,10,1]{2,1,0:T(8,128)S(1)} %get-tuple-element.237), channel_id=1, source_target_pairs={{32,0},{64,32},{96,64},{128,96},{160,128},{192,160},{224,192},{256... | collective-permute-start | bytes 2888 | tf_op jit(solution)/shard_map/ppermute | solution.py:23
  215.7 10.5 %collective-permute-start.28 = (f32[24,8,1]{2,1,0:T(8,128)S(1)}, f32[24,8,1]{2,1,0:T(8,128)S(1)}, u32[]{:S(2)}, u32[]{:S(2)}) collective-permute-start(f32[24,8,1]{2,1,0:T(8,128)S(1)} %get-tuple-element.281), channel_id=1, source_target_pairs={{0,32},{32,64},{64,96},{96,128},{128,160},{160,192},{192,224},{224... | collective-permute-start | bytes 2312 | tf_op jit(solution)/shard_map/ppermute | solution.py:21
  217.6 11.3 %collective-permute-start.29 = (f32[24,8,1]{2,1,0:T(8,128)S(1)}, f32[24,8,1]{2,1,0:T(8,128)S(1)}, u32[]{:S(2)}, u32[]{:S(2)}) collective-permute-start(f32[24,8,1]{2,1,0:T(8,128)S(1)} %get-tuple-element.282), channel_id=1, source_target_pairs={{32,0},{64,32},{96,64},{128,96},{160,128},{192,160},{224,192},{256... | collective-permute-start | bytes 2312 | tf_op jit(solution)/shard_map/ppermute | solution.py:23
  242.8 32.9 %collective-permute-start.32 = (f32[40,10,1]{2,1,0:T(8,128)S(1)}, f32[40,10,1]{2,1,0:T(8,128)S(1)}, u32[]{:S(2)}, u32[]{:S(2)}) collective-permute-start(f32[40,10,1]{2,1,0:T(8,128)S(1)} %get-tuple-element.236), channel_id=1, source_target_pairs={{0,32},{32,64},{64,96},{96,128},{128,160},{160,192},{192,224},{224... | collective-permute-start | bytes 4808 | tf_op jit(solution)/shard_map/ppermute | solution.py:21
  244.9 33.8 %collective-permute-start.33 = (f32[40,10,1]{2,1,0:T(8,128)S(1)}, f32[40,10,1]{2,1,0:T(8,128)S(1)}, u32[]{:S(2)}, u32[]{:S(2)}) collective-permute-start(f32[40,10,1]{2,1,0:T(8,128)S(1)} %get-tuple-element.235), channel_id=1, source_target_pairs={{32,0},{64,32},{96,64},{128,96},{160,128},{192,160},{224,192},{256... | collective-permute-start | bytes 4808 | tf_op jit(solution)/shard_map/ppermute | solution.py:23
  284.2 9.2 %collective-permute-start.34 = (f32[40,1,128]{2,1,0:T(1,128)S(1)}, f32[40,1,128]{2,1,0:T(1,128)S(1)}, u32[]{:S(2)}, u32[]{:S(2)}) collective-permute-start(f32[40,1,128]{2,1,0:T(1,128)S(1)} %get-tuple-element.248), channel_id=1, source_target_pairs={{0,1},{1,2},{2,3},{3,4},{4,5},{5,6},{6,7},{7,8},{8,9},{9,10},{10,1... | collective-permute-start | bytes 61448 | tf_op jit(solution)/shard_map/ppermute | solution.py:21
  (17 other events, 110.4 us)
where the time goes:
time: 302 us; the launch traced here: 301 us
  starting transfers between devices  156 us (52%)
  waiting for transfers between devices  113 us (37%)
  local copies, waits for them, and re-layouts  18.6 us (6%)
  other arithmetic  10.7 us (4%)
    ppermute x18, starting transfers between devices, extended_2(): lax.ppermute(head, axis, [((i + 1) % count, i) for i in range(ends)])  85.1 us
    ppermute x18, starting transfers between devices, extended_2(): lax.ppermute(tail, axis, [(i, (i + 1) % count) for i in range(ends)])  71 us
    ppermute x18, waiting for transfers between devices, extended_2(): lax.ppermute(tail, axis, [(i, (i + 1) % count) for i in range(ends)])  58.3 us
    ppermute x18, waiting for transfers between devices, extended_2(): lax.ppermute(head, axis, [((i + 1) % count, i) for i in range(ends)])  55.2 us
    scatter-add x4, local copies, waits for them, and re-layouts, return_rims(): inner_part.at[..., lon_cols - rim_width:].add(arrived[..., 3 * rim_width:])  10.8 us
  transfers between devices with their start and end apart: 36, of which 19 were waited for; matrix products, arithmetic and copies ran while one was open for 2% of the time, Pallas kernels for 0%

commit v1 on v0

v1 whole, which is shorter than its diff:
```python
import jax
import jax.numpy as jnp
from jax import lax
from jax.experimental import pallas as pl
from jax.experimental.pallas import tpu as pltpu
from jax.sharding import PartitionSpec as P

MESH = pl.DeviceIdType.MESH
STEPS = 4
HALO = 4
HORIZ = 0.22
VERT = 0.05

TRACER, COTAN, EAST, NORTH, COUNT, EASTWARD, WESTWARD, SLABS = 0, 24, 48, 56, 64, 65, 68, 71
ROWS = 32


def neighbour(north, east):
    lat, lon = lax.axis_index("lat"), lax.axis_index("lon")
    lats, lons = lax.axis_size("lat"), lax.axis_size("lon")
    return {"lat": lax.rem(lat + north + lats, lats), "lon": lax.rem(lon + east + lons, lons)}


def pack_columns(ext):
    lane = lax.broadcasted_iota(jnp.int32, (8, 128), 1)
    group = lane // HALO
    for plane in range(2):
        last = jnp.zeros((8, 128), jnp.float32)
        first = jnp.zeros((8, 128), jnp.float32)
        for slot in range(4):
            for level in range(8):
                place = 4 * level + slot
                field = ext[(4 * plane + slot) * 8 + level, 8:16, :]
                turned = pltpu.roll(field, (HALO * place + HALO) % 128, 1)
                last = jnp.where(group == place, turned, last)
                first = jnp.where(group == (place + 1) % 32, turned, first)
        ext[EASTWARD + plane, 8:16, :] = last
        ext[WESTWARD + plane, 8:16, :] = first
    turned = pltpu.roll(ext[COUNT, 8:16, :], HALO, 1)
    both = jnp.where(lane < 2 * HALO, turned, 0.0)
    for shift in (16, 32, 64):
        both = both + pltpu.roll(both, shift, 1)
    ext[EASTWARD + 2, 8:16, :] = both
    ext[WESTWARD + 2, 8:16, :] = both


def exchange_kernel(tracers, cotangent, east_vel, north_vel, sea_mask, level_count, ext, west, east, mask, count, load_sem, send_sem, recv_sem):
    around = [(a, b) for a in (-1, 0, 1) for b in (-1, 0, 1) if (a, b) != (0, 0)]
    barrier = pltpu.get_barrier_semaphore()
    for north, easterly in around:
        pl.semaphore_signal(barrier, inc=1, device_id=neighbour(north, easterly), device_id_type=MESH)
    loads = []
    for source, target in (
        (sea_mask, mask),
        (level_count, count),
        (tracers, ext.at[TRACER : TRACER + 24, 8:16, :]),
        (cotangent, ext.at[COTAN : COTAN + 24, 8:16, :]),
        (east_vel, ext.at[EAST : EAST + 8, 8:16, :]),
        (north_vel, ext.at[NORTH : NORTH + 8, 8:16, :]),
    ):
        loads.append(pltpu.make_async_copy(source, target, load_sem.at[len(loads)]))
        loads[-1].start()
    for load in loads:
        load.wait()
    ext[COUNT, 8:16, :] = jnp.where(mask[...] == 1, count[...], 0).astype(jnp.float32)
    pack_columns(ext)
    eastward, westward = slice(EASTWARD, EASTWARD + 3), slice(WESTWARD, WESTWARD + 3)
    plan = (
        (0, 1, ext.at[eastward, 8:16, :], west.at[:, 0:8, :]),
        (0, -1, ext.at[westward, 8:16, :], east.at[:, 0:8, :]),
        (1, 1, ext.at[eastward, 12:16, :], west.at[:, 12:16, :]),
        (-1, 1, ext.at[eastward, 8:12, :], west.at[:, 8:12, :]),
        (1, -1, ext.at[westward, 12:16, :], east.at[:, 12:16, :]),
        (-1, -1, ext.at[westward, 8:12, :], east.at[:, 8:12, :]),
        (1, 0, ext.at[:, 12:16, :], ext.at[:, 20:24, :]),
        (-1, 0, ext.at[:, 8:12, :], ext.at[:, 16:20, :]),
    )
    pl.semaphore_wait(barrier, len(around))
    copies = []
    for north, easterly, source, target in plan:
        copies.append(
            pltpu.make_async_remote_copy(
                src_ref=source,
                dst_ref=target,
                send_sem=send_sem.at[len(copies)],
                recv_sem=recv_sem.at[len(copies)],
                device_id=neighbour(north, easterly),
                device_id_type=MESH,
            )
        )
        copies[-1].start()
    for copy in copies:
        copy.wait_recv()
    for copy in copies:
        copy.wait_send()


def close_ring(ref, index, value):
    ref[index, 8:24, :] = value
    ref[index, 7:8, :] = value[15:16]
    ref[index, 24:25, :] = value[0:1]


def compute_kernel(ext, west, east, adj_tracers, adj_east, adj_north, strips, static, bridges, coefs, strip_coefs, states, sums, opens):
    shape = (16, 128)
    lane = lax.broadcasted_iota(jnp.int32, shape, 1)
    column = lane % 16
    level_of = (lane // 16).astype(jnp.float32)
    row = lax.broadcasted_iota(jnp.int32, shape, 0)
    lat, lats = lax.axis_index("lat"), lax.axis_size("lat")
    inside = ((row < 12) | (lat > 0)) & ((row < 8) | (row >= 12) | (lat < lats - 1))

    def turn(value, shift):
        return pltpu.roll(value, shift % 128, 1)

    def bridge(value):
        return jnp.where(column == 2, turn(value, -10), value)

    def join(quarters, slot):
        mine_last, mine_first, from_west, from_east = quarters
        joined = jnp.where(column < 4, turn(from_west, -4 * slot), turn(mine_first, -4 * slot))
        far = jnp.where(column < 12, turn(mine_last, 8 - 4 * slot), turn(from_east, 8 - 4 * slot))
        return jnp.where(column < 8, joined, far)

    for plane in range(3):
        quarters = (ext[EASTWARD + plane, 8:24, :], ext[WESTWARD + plane, 8:24, :], west[plane], east[plane])
        for slot in range(4 if plane < 2 else 1):
            field = 4 * plane + slot
            value = join(quarters, slot)
            if field < 6:
                close_ring(strips, field, value)
                bridges[field] = bridge(value)
            else:
                if field == 8:
                    value = jnp.where(inside, value, 0.0)
                close_ring(static, field - 6, value)

    counted = jnp.where(inside, ext[COUNT, 8:24, :], 0.0)
    close_ring(ext, COUNT, counted)
    ext[0:64, 7:8, :] = ext[0:64, 23:24, :]
    ext[0:64, 24:25, :] = ext[0:64, 8:9, :]

    def open_pair(is_open, velocity):
        half = velocity * 0.5
        return jnp.where(is_open, half + HORIZ, 0.0), jnp.where(is_open, half - HORIZ, 0.0)

    def stencil(wet, up, down, vel_east, vel_west, vel_north, vel_south, open_east, open_west, open_north, open_south):
        pe, qe = open_pair(open_east, vel_east)
        pw, qw = open_pair(open_west, vel_west)
        pn, qn = open_pair(open_north, vel_north)
        ps, qs = open_pair(open_south, vel_south)
        diagonal = jnp.where(wet, 1.0, 0.0) - pe + qw - pn + qs - up - down
        return diagonal, pe, pw, qe, qw, pn, ps, qn, qs, up, down

    cnt, vel_e, vel_n = static[2, 8:24, :], static[0, 8:24, :], static[1, 8:24, :]
    cnt_s, cnt_n = static[2, 7:23, :], static[2, 9:25, :]
    open_e = jnp.minimum(cnt, turn(cnt, -1))
    open_w = jnp.minimum(cnt, turn(cnt, 1))
    made = stencil(
        cnt > level_of,
        jnp.where(cnt > level_of + 1.0, VERT, 0.0),
        jnp.where((cnt > level_of) & (level_of > 0.0), VERT, 0.0),
        vel_e,
        turn(vel_e, 1),
        vel_n,
        static[1, 7:23, :],
        open_e > level_of,
        open_w > level_of,
        jnp.minimum(cnt, cnt_n) > level_of,
        jnp.minimum(cnt, cnt_s) > level_of,
    )
    for place, value in enumerate(made):
        strip_coefs[place] = value

    cnt_bridge = bridge(static[2, 8:24, :])
    cnt_bridge = turn(cnt_bridge, -3)
    vel_bridge = bridge(vel_e)
    cnt_e = jnp.where(lane == 127, cnt_bridge, turn(counted, -1))
    cnt_w = jnp.where(lane == 0, cnt_bridge, turn(counted, 1))
    least_e = jnp.minimum(counted, cnt_e)
    least_w = jnp.minimum(counted, cnt_w)
    least_n = jnp.minimum(counted, ext[COUNT, 9:25, :])
    least_s = jnp.minimum(counted, ext[COUNT, 7:23, :])

    for level in range(8):
        here = float(level)
        vel_e = ext[EAST + level, 8:24, :]
        vel_w = jnp.where(lane == 0, turn(vel_bridge, -(16 * level + 3)), turn(vel_e, 1))
        made = stencil(
            counted > here,
            jnp.where(counted > here + 1.0, VERT, 0.0),
            jnp.where(counted > here, VERT if level else 0.0, 0.0),
            vel_e,
            vel_w,
            ext[NORTH + level, 8:24, :],
            ext[NORTH + level, 7:23, :],
            least_e > here,
            least_w > here,
            least_n > here,
            least_s > here,
        )
        for place, value in enumerate(made):
            coefs[level, place] = value
        opens[0, level] = jnp.where(least_e[0:8] > here, 0.5, 0.0)
        opens[1, level] = jnp.where(least_n[0:8] > here, 0.5, 0.0)

    def strip_step(source, target, names, base):
        d, e, w, n, s, up, down = (strip_coefs[name] for name in names)
        if names is FORWARD:
            e, n = -e, -n
        else:
            w, s = -w, -s
        for tracer in range(3):
            value = source[base + tracer, 8:24, :]
            result = (
                d * value
                + e * turn(value, -1)
                + w * turn(value, 1)
                + n * source[base + tracer, 9:25, :]
                + s * source[base + tracer, 7:23, :]
                + up * turn(value, -16)
                + down * turn(value, 16)
            )
            close_ring(target, base + tracer, result)
            bridges[base + tracer] = bridge(result)

    def sides(value, base, tracer, level, rows):
        edge = pltpu.roll(bridges[base + tracer], (128 - 3) - 16 * level, 1)[:rows]
        after = jnp.where(lane[:rows] == 127, edge, turn(value, -1))
        before = jnp.where(lane[:rows] == 0, edge, turn(value, 1))
        return after, before

    def forward_step(step):
        source = ext if step == 0 else states
        origin = TRACER if step == 0 else 24 * (step - 1)
        for level in range(8):
            d, e, w, n, s, up, down = (coefs[level, name] for name in FORWARD)
            for tracer in range(3):
                slab = origin + 8 * tracer + level
                value = source[slab, 8:24, :]
                north, south = source[slab, 9:25, :], source[slab, 7:23, :]
                after, before = sides(value, 0, tracer, level, 16)
                result = d * value - e * after + w * before - n * north + s * south
                if level < 7:
                    result = result + up * source[slab + 1, 8:24, :]
                if level > 0:
                    result = result + down * source[slab - 1, 8:24, :]
                close_ring(states, 24 * step + 8 * tracer + level, result)
                sums[step, 0, 8 * tracer + level] = value[:8] + after[:8]
                sums[step, 1, 8 * tracer + level] = value[:8] + north[:8]

    def last_sums():
        for level in range(8):
            for tracer in range(3):
                slab = 48 + 8 * tracer + level
                value = states[slab, 8:16, :]
                after, before = sides(value, 0, tracer, level, 8)
                sums[3, 0, 8 * tracer + level] = value + after
                sums[3, 1, 8 * tracer + level] = value + states[slab, 9:17, :]

    for step in range(3):
        forward_step(step)
        strip_step(strips, strips, FORWARD, 0)
    last_sums()

    def adjoint_step(step):
        source = ext if step == 0 else states
        origin = COTAN if step == 0 else 24 * (step - 1)
        rows = 16 if step < 3 else 8
        for level in range(8):
            d, e, w, n, s, up, down = (coefs[level, name, :rows] for name in ADJOINT)
            grad_e = jnp.zeros((8, 128), jnp.float32)
            grad_n = jnp.zeros((8, 128), jnp.float32)
            for tracer in range(3):
                slab = origin + 8 * tracer + level
                value = source[slab, 8 : 8 + rows, :]
                north, south = source[slab, 9 : 9 + rows, :], source[slab, 7 : 7 + rows, :]
                after, before = sides(value, 3, tracer, level, rows)
                result = d * value + e * after - w * before + n * north - s * south
                if level < 7:
                    result = result + up * source[slab + 1, 8 : 8 + rows, :]
                if level > 0:
                    result = result + down * source[slab - 1, 8 : 8 + rows, :]
                if step < 3:
                    close_ring(states, 24 * step + 8 * tracer + level, result)
                else:
                    adj_tracers[8 * tracer + level] = result
                grad_e = grad_e + sums[3 - step, 0, 8 * tracer + level] * (after[:8] - value[:8])
                grad_n = grad_n + sums[3 - step, 1, 8 * tracer + level] * (north[:8] - value[:8])
            if step > 0:
                grad_e = grad_e + adj_east[level]
                grad_n = grad_n + adj_north[level]
            if step == 3:
                grad_e = grad_e * opens[0, level]
                grad_n = grad_n * opens[1, level]
            adj_east[level] = grad_e
            adj_north[level] = grad_n

    for step in range(4):
        adjoint_step(step)
        if step < 3:
            strip_step(strips, strips, ADJOINT, 3)


FORWARD = (0, 3, 2, 7, 6, 9, 10)
ADJOINT = (0, 1, 4, 5, 8, 9, 10)


def on_device(tracers, cotangent, east_vel, north_vel, sea_mask, level_count):
    f32 = jnp.float32
    hbm = pl.BlockSpec(memory_space=pltpu.HBM)
    anywhere = pl.BlockSpec(memory_space=pl.ANY)
    vmem = pl.BlockSpec(memory_space=pltpu.VMEM)
    exchanged = pl.pallas_call(
        exchange_kernel,
        name="exchange",
        out_shape=(
            jax.ShapeDtypeStruct((SLABS, ROWS, 128), f32),
            jax.ShapeDtypeStruct((3, 16, 128), f32),
            jax.ShapeDtypeStruct((3, 16, 128), f32),
        ),
        in_specs=[hbm] * 6,
        out_specs=(vmem,) * 3,
        scratch_shapes=[
            pltpu.VMEM((8, 128), jnp.int32),
            pltpu.VMEM((8, 128), jnp.int32),
            pltpu.SemaphoreType.DMA((6,)),
            pltpu.SemaphoreType.DMA((8,)),
            pltpu.SemaphoreType.DMA((8,)),
        ],
        compiler_params=pltpu.CompilerParams(collective_id=0, has_side_effects=True, vmem_limit_bytes=8 << 20),
    )(*(pltpu.with_memory_space_constraint(x, pltpu.HBM) for x in (tracers.reshape(24, 8, 128), cotangent.reshape(24, 8, 128), east_vel, north_vel, sea_mask, level_count)))
    adj_tracers, adj_east, adj_north = pl.pallas_call(
        compute_kernel,
        name="compute",
        out_shape=(
            jax.ShapeDtypeStruct((24, 8, 128), f32),
            jax.ShapeDtypeStruct((8, 8, 128), f32),
            jax.ShapeDtypeStruct((8, 8, 128), f32),
        ),
        in_specs=[vmem] * 3,
        out_specs=(vmem,) * 3,
        scratch_shapes=[
            pltpu.VMEM((6, ROWS, 128), f32),
            pltpu.VMEM((3, ROWS, 128), f32),
            pltpu.VMEM((6, 16, 128), f32),
            pltpu.VMEM((8, 11, 16, 128), f32),
            pltpu.VMEM((11, 16, 128), f32),
            pltpu.VMEM((72, ROWS, 128), f32),
            pltpu.VMEM((4, 2, 24, 8, 128), f32),
            pltpu.VMEM((2, 8, 8, 128), f32),
        ],
        compiler_params=pltpu.CompilerParams(vmem_limit_bytes=16 << 20),
    )(*exchanged)
    return adj_tracers.reshape(tracers.shape), adj_east, adj_north


def solution(mesh):
    placed = (
        P(None, None, "lat", "lon"),
        P(None, None, "lat", "lon"),
        P(None, "lat", "lon"),
        P(None, "lat", "lon"),
        P("lat", "lon"),
        P("lat", "lon"),
    )
    return jax.shard_map(
        on_device,
        mesh=mesh,
        in_specs=placed,
        out_specs=(P(None, None, "lat", "lon"), P(None, "lat", "lon"), P(None, "lat", "lon")),
        check_vma=False,
    )
```

time: 302 us -> 30 us (0.10)
  the two profiles are of different devices: /device:TPU:59 before, /device:TPU:1 now
where the time goes in v1:
time: 30 us; the launch traced here: 29.9 us
  Pallas kernels  29.2 us (97%)
  between operations  0.64 us (2%)
    pallas_call x1, Pallas kernels, on_device(): pl.pallas_call(exchange_kernel, name='exchange', out_shape=(jax.ShapeDtyp...  25.7 us
    pallas_call x1, Pallas kernels, on_device(): pl.pallas_call(compute_kernel, name='compute', out_shape=(jax.ShapeDtypeS...  3.52 us

profile of v1, /device:TPU:1, one launch (start us, length us, event | category | flops | bytes accessed | tf_op | source)
XLA Modules:
  0.0 29.9 jit_solution(2157373834018131048)
XLA Ops:
  0.6 25.7 %exchange.1 = (f32[71,32,128]{2,1,0:T(8,128)S(1)}, f32[3,16,128]{2,1,0:T(8,128)S(1)}, f32[3,16,128]{2,1,0:T(8,128)S(1)}) custom-call(f32[24,8,128]{2,1,0:T(8,128)} %bitcast.3, f32[24,8,128]{2,1,0:T(8,128)} %bitcast.4, f32[8,8,128]{2,1,0:T(8,128)} %east_vel.1, f32[8,8,128]{2,1,0:T(8,128)} %north_vel.1, s32[8,128]{1,0:T(8,128)} %sea_mask.1, s32[8,128]{1,0:T(8,128)} %level_count.1), custom_call_target="tpu_custom_call" | custom-call | tf_op jit(solution)/shard_map/exchange/pallas_call | solution.py:314
  26.4 3.5 %compute.1 = (f32[24,8,128]{2,1,0:T(8,128)}, f32[8,8,128]{2,1,0:T(8,128)}, f32[8,8,128]{2,1,0:T(8,128)}) custom-call(f32[71,32,128]{2,1,0:T(8,128)S(1)} %get-tuple-element.9.ext, f32[3,16,128]{2,1,0:T(8,128)S(1)} %get-tuple-element.10.west, f32[3,16,128]{2,1,0:T(8,128)S(1)} %get-tuple-element.11.east), custom_call_target="tpu_custom_call" | custom-call | tf_op jit(solution)/shard_map/compute/pallas_call | solution.py:333

commit v2 on v0

v2 whole, which is shorter than its diff:
```python
import jax
import jax.numpy as jnp
from jax import lax
from jax.experimental import pallas as pl
from jax.experimental.pallas import tpu as pltpu
from jax.sharding import PartitionSpec as P

MESH = pl.DeviceIdType.MESH
HALO = 4
HORIZ = 0.22
VERT = 0.05
LEVELS = 8
TRACERS = 3
UNROLL = 2

TRACER, COTAN, EAST, NORTH, COUNT, PLANES = 0, 24, 48, 56, 64, 65
ROWS = 32
STRIPS = 17
FORWARD = (0, 3, 2, 7, 6, 9, 10)
ADJOINT = (0, 1, 4, 5, 8, 9, 10)


def turn(value, shift):
    return pltpu.roll(value, shift % 128, 1)


def lanes_of(rows):
    return lax.broadcasted_iota(jnp.int32, (rows, 128), 1)


def inside_grid():
    row = lax.broadcasted_iota(jnp.int32, (16, 128), 0)
    lat, lats = lax.axis_index("lat"), lax.axis_size("lat")
    return ((row < 12) | (lat > 0)) & ((row < 8) | (row >= 12) | (lat < lats - 1))


def close_ring(ref, index, value):
    ref[index, 8:24, :] = value
    ref[index, 7:8, :] = value[15:16]
    ref[index, 24:25, :] = value[0:1]


def open_pair(is_open, velocity):
    half = velocity * 0.5
    return jnp.where(is_open, half + HORIZ, 0.0), jnp.where(is_open, half - HORIZ, 0.0)


def stencil(wet, up, down, vel_east, vel_west, vel_north, vel_south, open_east, open_west, open_north, open_south):
    pe, qe = open_pair(open_east, vel_east)
    pw, qw = open_pair(open_west, vel_west)
    pn, qn = open_pair(open_north, vel_north)
    ps, qs = open_pair(open_south, vel_south)
    diagonal = jnp.where(wet, 1.0, 0.0) - pe + qw - pn + qs - up - down
    return diagonal, pe, pw, qe, qw, pn, ps, qn, qs, up, down


def neighbour(north, east):
    lat, lon = lax.axis_index("lat"), lax.axis_index("lon")
    lats, lons = lax.axis_size("lat"), lax.axis_size("lon")
    return {"lat": lax.rem(lat + north + lats, lats), "lon": lax.rem(lon + east + lons, lons)}


def greetings(side):
    place, places = lax.axis_index("lon"), lax.axis_size("lon")
    if places < 3:
        return place >= 0, place >= 0
    if side > 0:
        return (place != places - 1) & (place != places - 2), place >= 0
    return place >= 0, (place != places - 1) & (place != 0)


def pack_ends(ext, packed):
    group = lanes_of(8) // HALO
    for half in range(2):
        last = jnp.zeros((8, 128), jnp.float32)
        first = jnp.zeros((8, 128), jnp.float32)
        for field in range(8):
            for i in range(4):
                place = 8 * i + field
                turned = turn(ext[8 * field + 2 * i + half, 8:16, :], HALO * (place + 1))
                last = jnp.where(group == place, turned, last)
                first = jnp.where(group == (place + 1) % 32, turned, first)
        packed[half] = last
        packed[3 + half] = first
    both = jnp.where(group < 2, turn(ext[COUNT, 8:16, :], HALO), 0.0)
    for shift in (32, 64):
        both = both + turn(both, shift)
    packed[2] = both
    packed[5] = both


def pack_strips(ext, own):
    lane = lanes_of(16)
    group, place = lane // 32, lane % 32

    def spread(value):
        return jnp.where(place < 12, turn(value, -12), turn(value, 4))

    for field in range(8):
        for half in range(2):
            gathered = jnp.zeros((16, 128), jnp.float32)
            for i in range(4):
                turned = turn(ext[8 * field + 2 * i + half, 8:24, :], 32 * i + 16)
                gathered = jnp.where(group == i, turned, gathered)
            own[2 * field + half] = spread(gathered)
    gathered = jnp.where(lane < 32, turn(ext[COUNT, 8:24, :], 16), 0.0)
    for shift in (32, 64):
        gathered = gathered + turn(gathered, shift)
    own[16] = spread(gathered)


def exchange_kernel(
    tracers, cotangent, east_vel, north_vel, sea_mask, level_count,
    adj_tracers, adj_east, adj_north, own, west, east,
    ext, packed, mask, count, coefs, opens, states, sums, load_sem, send_sem, recv_sem, answer_sem,
):
    loads = []
    for source, target in (
        (tracers, ext.at[TRACER : TRACER + 24, 8:16, :]),
        (cotangent, ext.at[COTAN : COTAN + 24, 8:16, :]),
        (east_vel, ext.at[EAST : EAST + 8, 8:16, :]),
        (north_vel, ext.at[NORTH : NORTH + 8, 8:16, :]),
        (sea_mask, mask),
        (level_count, count),
    ):
        loads.append(pltpu.make_async_copy(source, target, load_sem.at[len(loads)]))
        loads[-1].start()

    lat, lats, lon, lons = lax.axis_index("lat"), lax.axis_size("lat"), lax.axis_index("lon"), lax.axis_size("lon")
    exists = {0: lat >= 0, 1: lat < lats - 1, -1: lat > 0}
    barrier = pltpu.get_barrier_semaphore()
    in_column = jnp.where(exists[1], 1, 0) + jnp.where(exists[-1], 1, 0)
    expected = in_column
    for side in (-1, 1):
        greets, greeted = greetings(side)
        expected = expected + jnp.where(greeted, in_column + 1, 0)
        for north in (0, 1, -1):

            @pl.when(greets & exists[north])
            def _():
                pl.semaphore_signal(barrier, inc=1, device_id=neighbour(north, side), device_id_type=MESH)

    for north in (1, -1):

        @pl.when(exists[north])
        def _():
            pl.semaphore_signal(barrier, inc=1, device_id=neighbour(north, 0), device_id_type=MESH)

    for north, rows in ((1, slice(8, 12)), (-1, slice(12, 16))):

        @pl.when(~exists[north])
        def _():
            west[:, rows, :] = jnp.zeros((3, 4, 128), jnp.float32)
            east[:, rows, :] = jnp.zeros((3, 4, 128), jnp.float32)
            ext[:, rows.start + 8 : rows.stop + 8, :] = jnp.zeros((PLANES, 4, 128), jnp.float32)

    plan = (
        (0, 1, packed.at[0:3], west.at[:, 0:8, :]),
        (1, 1, packed.at[0:3, 4:8, :], west.at[:, 12:16, :]),
        (-1, 1, packed.at[0:3, 0:4, :], west.at[:, 8:12, :]),
        (0, -1, packed.at[3:6], east.at[:, 0:8, :]),
        (1, -1, packed.at[3:6, 4:8, :], east.at[:, 12:16, :]),
        (-1, -1, packed.at[3:6, 0:4, :], east.at[:, 8:12, :]),
        (1, 0, ext.at[:, 12:16, :], ext.at[:, 20:24, :]),
        (-1, 0, ext.at[:, 8:12, :], ext.at[:, 16:20, :]),
    )
    copies = []
    for north, easterly, source, target in plan:
        copy = pltpu.make_async_remote_copy(
            src_ref=source,
            dst_ref=target,
            send_sem=send_sem.at[len(copies)],
            recv_sem=recv_sem.at[len(copies)],
            device_id=neighbour(north, easterly),
            device_id_type=MESH,
        )
        copies.append((copy, exists[north], exists[-north]))

    def start(chosen, condition):
        for copy, sent, _ in chosen:
            pl.when(sent & condition)(copy.start)

    def wait_recv(chosen):
        for copy, _, received in chosen:
            pl.when(received)(copy.wait_recv)

    def answer(side, theirs):
        for north in (0, 1, -1):

            @pl.when(~greetings(side)[0] & exists[north])
            def _():
                pl.semaphore_signal(theirs, inc=1, device_id=neighbour(north, side), device_id_type=MESH)

    eastward, westward, along = copies[0:3], copies[3:6], copies[6:8]
    first, last = lon == 0, lon == lons - 1
    pl.semaphore_wait(barrier, expected)
    answer(1, answer_sem.at[0])
    for load in loads:
        load.wait()
    ext[COUNT, 8:16, :] = jnp.where(mask[...] == 1, count[...], 0).astype(jnp.float32)
    pack_ends(ext, packed)
    start(eastward, lon >= 0)
    greeted = greetings(-1)[1]
    start(westward, greeted)
    start(along, lon >= 0)

    def start_answered(condition):
        @pl.when(condition)
        def _():
            pl.semaphore_wait(answer_sem.at[0], in_column + 1)

        start(westward, condition)

    start_answered(~greeted & last)
    wait_recv(along)
    interior(ext, adj_tracers, adj_east, adj_north, coefs, opens, states, sums)
    pack_strips(ext, own)
    start_answered(~greeted & first)
    wait_recv(eastward)
    wait_recv(westward)
    for copy, sent, _ in copies:
        pl.when(sent)(copy.wait_send)


def interior(ext, adj_tracers, adj_east, adj_north, coefs, opens, states, sums):
    margins = jnp.where(inside_grid()[8:16], ext[COUNT, 16:24, :], 0.0)
    ext[COUNT, 16:24, :] = margins
    ext[COUNT, 7:8, :] = margins[7:8]
    ext[COUNT, 24:25, :] = ext[COUNT, 8:9, :]

    def each_level(body):
        def step(level, carry):
            body(level)
            return carry

        lax.fori_loop(0, LEVELS, step, 0, unroll=UNROLL)

    def repeat_ends(level):
        for field in range(8):
            ext[8 * field + level, 7:8, :] = ext[8 * field + level, 23:24, :]
            ext[8 * field + level, 24:25, :] = ext[8 * field + level, 8:9, :]

    each_level(repeat_ends)

    def coefficients(level):
        here = level.astype(jnp.float32)
        cnt = ext[COUNT, 8:24, :]
        vel_e = ext[EAST + level, 8:24, :]
        open_e = jnp.minimum(cnt, turn(cnt, -1)) > here
        open_n = jnp.minimum(cnt, ext[COUNT, 9:25, :]) > here
        made = stencil(
            cnt > here,
            jnp.where(cnt > here + 1.0, VERT, 0.0),
            jnp.where(cnt > here, jnp.where(level > 0, VERT, 0.0), 0.0),
            vel_e,
            turn(vel_e, 1),
            ext[NORTH + level, 8:24, :],
            ext[NORTH + level, 7:23, :],
            open_e,
            jnp.minimum(cnt, turn(cnt, 1)) > here,
            open_n,
            jnp.minimum(cnt, ext[COUNT, 7:23, :]) > here,
        )
        for place, value in enumerate(made):
            coefs[level, place] = value
        opens[level, 0] = jnp.where(open_e[0:8], 0.5, 0.0)
        opens[level, 1] = jnp.where(open_n[0:8], 0.5, 0.0)

    each_level(coefficients)

    def near(source, origin, tracer, level, rows):
        base = origin + LEVELS * tracer
        value = source[base + level, 8 : 8 + rows, :]
        north, south = source[base + level, 9 : 9 + rows, :], source[base + level, 7 : 7 + rows, :]
        above = source[base + jnp.minimum(level + 1, LEVELS - 1), 8 : 8 + rows, :]
        below = source[base + jnp.maximum(level - 1, 0), 8 : 8 + rows, :]
        return value, turn(value, -1), turn(value, 1), north, south, above, below

    def forward_step(step, level):
        source = ext if step == 0 else states
        origin = TRACER if step == 0 else 24 * (step - 1)
        d, e, w, n, s, up, down = (coefs[level, name] for name in FORWARD)
        for tracer in range(TRACERS):
            value, after, before, north, south, above, below = near(source, origin, tracer, level, 16)
            result = d * value - e * after + w * before - n * north + s * south + up * above + down * below
            close_ring(states, 24 * step + LEVELS * tracer + level, result)
            sums[step, 0, LEVELS * tracer + level] = value[:8] + after[:8]
            sums[step, 1, LEVELS * tracer + level] = value[:8] + north[:8]

    def last_sums(level):
        for tracer in range(TRACERS):
            slab = 48 + LEVELS * tracer + level
            value = states[slab, 8:16, :]
            sums[3, 0, LEVELS * tracer + level] = value + turn(value, -1)
            sums[3, 1, LEVELS * tracer + level] = value + states[slab, 9:17, :]

    def adjoint_step(step, level):
        source = ext if step == 0 else states
        origin = COTAN if step == 0 else 24 * (step - 1)
        rows = 16 if step < 3 else 8
        d, e, w, n, s, up, down = (coefs[level, name, :rows] for name in ADJOINT)
        grad_e = jnp.zeros((8, 128), jnp.float32)
        grad_n = jnp.zeros((8, 128), jnp.float32)
        for tracer in range(TRACERS):
            value, after, before, north, south, above, below = near(source, origin, tracer, level, rows)
            result = d * value + e * after - w * before + n * north - s * south + up * above + down * below
            if step < 3:
                close_ring(states, 24 * step + LEVELS * tracer + level, result)
            else:
                adj_tracers[LEVELS * tracer + level] = result
            grad_e = grad_e + sums[3 - step, 0, LEVELS * tracer + level] * (after[:8] - value[:8])
            grad_n = grad_n + sums[3 - step, 1, LEVELS * tracer + level] * (north[:8] - value[:8])
        if step > 0:
            grad_e = grad_e + adj_east[level]
            grad_n = grad_n + adj_north[level]
        if step == 3:
            grad_e = grad_e * opens[level, 0]
            grad_n = grad_n * opens[level, 1]
        adj_east[level] = grad_e
        adj_north[level] = grad_n

    for step in range(3):
        each_level(lambda level, step=step: forward_step(step, level))
    each_level(last_sums)
    for step in range(4):
        each_level(lambda level, step=step: adjoint_step(step, level))


def ends_kernel(part_tracers, part_east, part_north, own, west, east, adj_tracers, adj_east, adj_north, rings):
    lane = lanes_of(16)
    place = lane % 32
    inside = inside_grid()

    def joined(field, half):
        index = 2 * field + half
        source = half if field < 8 else 2
        shift = 4 * field if field < 8 else 0
        value = jnp.where(place < 4, turn(west[source], -shift), own[index])
        return jnp.where((place >= 20) & (place < 24), turn(east[source], 16 - shift), value)

    def stored(field, half, value):
        close_ring(rings, 2 * field + half, value)
        return value

    count = stored(8, 0, jnp.where(inside, joined(8, 0), 0.0))
    counts = (count, turn(count, -1), turn(count, 1), rings[16, 9:25, :], rings[16, 7:23, :])
    least = [jnp.minimum(count, other) for other in counts]
    made, opens = [], []
    for half in range(2):
        level = (2 * (lane // 32) + half).astype(jnp.float32)
        vel_e = joined(6, half)
        vel_n = stored(7, half, joined(7, half))
        opened = [value > level for value in least]
        made.append(
            stencil(
                opened[0],
                jnp.where(count > level + 1.0, VERT, 0.0),
                jnp.where(opened[0] & (level > 0.0), VERT, 0.0),
                vel_e,
                turn(vel_e, 1),
                vel_n,
                rings[14 + half, 7:23, :],
                *opened[1:],
            )
        )
        opens.append([jnp.where(opened[which][:8], 0.5, 0.0) for which in (1, 3)])

    def advanced(field, values, names, rows):
        near = []
        for half in range(2):
            value = values[half]
            ring = 2 * field + half
            near.append((value, turn(value, -1), turn(value, 1), rings[ring, 9 : 9 + rows, :], rings[ring, 7 : 7 + rows, :]))
        results = []
        for half in range(2):
            value, after, before, north, south = near[half]
            d, e, w, n, s, up, down = (made[half][name][:rows] for name in names)
            above = values[1] if half == 0 else turn(values[0], -32)
            below = turn(values[1], 32) if half == 0 else values[0]
            if names is FORWARD:
                result = d * value - e * after + w * before - n * north + s * south
            else:
                result = d * value + e * after - w * before + n * north - s * south
            results.append(result + up * above + down * below)
        return results, near

    fields = [[stored(field, half, joined(field, half)) for half in range(2)] for field in range(6)]
    sums = []
    for step in range(4):
        sums.append([])
        for tracer in range(TRACERS):
            if step < 3:
                results, near = advanced(tracer, fields[tracer], FORWARD, 16)
            else:
                results = fields[tracer]
                near = [(value, turn(value, -1), None, rings[2 * tracer + half, 9:25, :]) for half, value in enumerate(results)]
            sums[step].append([(value[:8] + after[:8], value[:8] + north[:8]) for value, after, _, north, *_ in near])
            if step < 3:
                fields[tracer] = [stored(tracer, half, value) for half, value in enumerate(results)]
    grads = [[jnp.zeros((8, 128), jnp.float32)] * 2 for half in range(2)]
    for step in range(4):
        for tracer in range(TRACERS):
            rows = 16 if step < 3 else 8
            values = [value[:rows] for value in fields[3 + tracer]]
            results, near = advanced(3 + tracer, values, ADJOINT, rows)
            for half in range(2):
                value, after, _, north, _ = near[half]
                east_sum, north_sum = sums[3 - step][tracer][half]
                grads[half] = [
                    grads[half][0] + east_sum * (after[:8] - value[:8]),
                    grads[half][1] + north_sum * (north[:8] - value[:8]),
                ]
            fields[3 + tracer] = [stored(3 + tracer, half, value) if step < 3 else value for half, value in enumerate(results)]

    short = lanes_of(8)
    at_end = (short < 4) | (short >= 124)
    short_place = short % 32

    def patched(value, part, target, half, base):
        value = jnp.where(short_place < 4, turn(value, -16), value)
        for i in range(4):
            slab = base + 2 * i + half
            target[slab] = jnp.where(at_end, turn(value, -(32 * i + 4)), part[slab])

    for half in range(2):
        for tracer in range(TRACERS):
            patched(fields[3 + tracer][half], part_tracers, adj_tracers, half, LEVELS * tracer)
        patched(grads[half][0] * opens[half][0], part_east, adj_east, half, 0)
        patched(grads[half][1] * opens[half][1], part_north, adj_north, half, 0)


def on_device(tracers, cotangent, east_vel, north_vel, sea_mask, level_count):
    f32 = jnp.float32
    vmem = pl.BlockSpec(memory_space=pltpu.VMEM)
    operands = (tracers.reshape(24, 8, 128), cotangent.reshape(24, 8, 128), east_vel, north_vel, sea_mask, level_count)
    results = (
        jax.ShapeDtypeStruct((24, 8, 128), f32),
        jax.ShapeDtypeStruct((8, 8, 128), f32),
        jax.ShapeDtypeStruct((8, 8, 128), f32),
    )
    parts = pl.pallas_call(
        exchange_kernel,
        name="exchange",
        out_shape=(
            *results,
            jax.ShapeDtypeStruct((STRIPS, 16, 128), f32),
            jax.ShapeDtypeStruct((3, 16, 128), f32),
            jax.ShapeDtypeStruct((3, 16, 128), f32),
        ),
        in_specs=[pl.BlockSpec(memory_space=pltpu.HBM)] * 6,
        out_specs=(vmem,) * 6,
        scratch_shapes=[
            pltpu.VMEM((PLANES, ROWS, 128), f32),
            pltpu.VMEM((6, 8, 128), f32),
            pltpu.VMEM((8, 128), jnp.int32),
            pltpu.VMEM((8, 128), jnp.int32),
            pltpu.VMEM((LEVELS, 11, 16, 128), f32),
            pltpu.VMEM((LEVELS, 2, 8, 128), f32),
            pltpu.VMEM((72, ROWS, 128), f32),
            pltpu.VMEM((4, 2, 24, 8, 128), f32),
            pltpu.SemaphoreType.DMA((6,)),
            pltpu.SemaphoreType.DMA((8,)),
            pltpu.SemaphoreType.DMA((8,)),
            pltpu.SemaphoreType.REGULAR((1,)),
        ],
        compiler_params=pltpu.CompilerParams(collective_id=0, has_side_effects=True, vmem_limit_bytes=16 << 20),
    )(*(pltpu.with_memory_space_constraint(operand, pltpu.HBM) for operand in operands))
    adj_tracers, adj_east, adj_north = pl.pallas_call(
        ends_kernel,
        name="ends",
        out_shape=results,
        in_specs=[vmem] * 6,
        out_specs=(vmem,) * 3,
        scratch_shapes=[pltpu.VMEM((STRIPS, ROWS, 128), f32)],
        compiler_params=pltpu.CompilerParams(vmem_limit_bytes=16 << 20),
    )(*parts)
    return adj_tracers.reshape(tracers.shape), adj_east, adj_north


def solution(mesh):
    placed = (
        P(None, None, "lat", "lon"),
        P(None, None, "lat", "lon"),
        P(None, "lat", "lon"),
        P(None, "lat", "lon"),
        P("lat", "lon"),
        P("lat", "lon"),
    )
    return jax.shard_map(
        on_device,
        mesh=mesh,
        in_specs=placed,
        out_specs=(P(None, None, "lat", "lon"), P(None, "lat", "lon"), P(None, "lat", "lon")),
        check_vma=False,
    )
```

time: 302 us -> 25 us (0.08)
  the two profiles are of different devices: /device:TPU:59 before, /device:TPU:1 now
where the time goes in v2:
time: 25 us; the launch traced here: 24.8 us
  Pallas kernels  24.2 us (97%)
  between operations  0.64 us (3%)
    pallas_call x1, Pallas kernels, on_device(): pl.pallas_call(exchange_kernel, name='exchange', out_shape=(*results, jax...  22.8 us
    pallas_call x1, Pallas kernels, on_device(): pl.pallas_call(ends_kernel, name='ends', out_shape=results, in_specs=[vme...  1.36 us

profile of v2, /device:TPU:1, one launch (start us, length us, event | category | flops | bytes accessed | tf_op | source)
XLA Modules:
  0.0 24.8 jit_solution(9354107018675413074)
XLA Ops:
  0.6 22.8 %exchange.1 = (f32[24,8,128]{2,1,0:T(8,128)S(1)}, f32[8,8,128]{2,1,0:T(8,128)S(1)}, f32[8,8,128]{2,1,0:T(8,128)S(1)}, f32[17,16,128]{2,1,0:T(8,128)S(1)}, f32[3,...) custom-call(f32[24,8,128]{2,1,0:T(8,128)} %bitcast.3, f32[24,8,128]{2,1,0:T(8,128)} %bitcast.4, f32[8,8,128]{2,1,0:T(8,128)} %east_vel.1, ...), custom_call_target="tpu_custom_call" | custom-call | tf_op jit(solution)/shard_map/exchange/pallas_call | solution.py:441
  23.4 1.4 %ends.1 = (f32[24,8,128]{2,1,0:T(8,128)}, f32[8,8,128]{2,1,0:T(8,128)}, f32[8,8,128]{2,1,0:T(8,128)}) custom-call(f32[24,8,128]{2,1,0:T(8,128)S(1)} %get-tuple-element.12.part_tracers, f32[8,8,128]{2,1,0:T(8,128)S(1)} %get-tuple-element.13.part_east, f32[8,8,128]{2,1,0:T(8,128)S(1)} %get-tuple-element.14.part_north, ...), custom_call_target="tpu_custom_call" | custom-call | tf_op jit(solution)/shard_map/ends/pallas_call | solution.py:468

commit v3 on v2

--- a/solution.py
+++ b/solution.py
@@ -15,7 +15,8 @@
 
 TRACER, COTAN, EAST, NORTH, COUNT, PLANES = 0, 24, 48, 56, 64, 65
 ROWS = 32
-STRIPS = 17
+STRIPS = 9
+SPARE = (0, 1, 2, 7)
 FORWARD = (0, 3, 2, 7, 6, 9, 10)
 ADJOINT = (0, 1, 4, 5, 8, 9, 10)
 
@@ -26,12 +27,6 @@
 
 def lanes_of(rows):
     return lax.broadcasted_iota(jnp.int32, (rows, 128), 1)
-
-
-def inside_grid():
-    row = lax.broadcasted_iota(jnp.int32, (16, 128), 0)
-    lat, lats = lax.axis_index("lat"), lax.axis_size("lat")
-    return ((row < 12) | (lat > 0)) & ((row < 8) | (row >= 12) | (lat < lats - 1))
 
 
 def close_ring(ref, index, value):
@@ -54,10 +49,12 @@
     return diagonal, pe, pw, qe, qw, pn, ps, qn, qs, up, down
 
 
-def neighbour(north, east):
+def neighbours():
     lat, lon = lax.axis_index("lat"), lax.axis_index("lon")
-    lats, lons = lax.axis_size("lat"), lax.axis_size("lon")
-    return {"lat": lax.rem(lat + north + lats, lats), "lon": lax.rem(lon + east + lons, lons)}
+    last_lat, last_lon = lax.axis_size("lat") - 1, lax.axis_size("lon") - 1
+    lats = {0: lat, 1: jnp.where(lat == last_lat, 0, lat + 1), -1: jnp.where(lat == 0, last_lat, lat - 1)}
+    lons = {0: lon, 1: jnp.where(lon == last_lon, 0, lon + 1), -1: jnp.where(lon == 0, last_lon, lon - 1)}
+    return lambda north, east: {"lat": lats[north], "lon": lons[east]}
 
 
 def greetings(side):
@@ -70,7 +67,15 @@
 
 
 def pack_ends(ext, packed):
-    group = lanes_of(8) // HALO
+    lane = lanes_of(8)
+    group = lane // HALO
+    counts = ext[COUNT, 8:16, :]
+    spread = jnp.zeros((8, 128), jnp.float32)
+    for column, field in enumerate(SPARE):
+        spread = jnp.where(lane == HALO * field, turn(counts, HALO * field - 124 - column), spread)
+    for shift in (32, 64):
+        spread = spread + turn(spread, shift)
+    is_spare = (lane % 32 == 0) | (lane % 32 == 4) | (lane % 32 == 8) | (lane % 32 == 28)
     for half in range(2):
         last = jnp.zeros((8, 128), jnp.float32)
         first = jnp.zeros((8, 128), jnp.float32)
@@ -80,39 +85,115 @@
                 turned = turn(ext[8 * field + 2 * i + half, 8:16, :], HALO * (place + 1))
                 last = jnp.where(group == place, turned, last)
                 first = jnp.where(group == (place + 1) % 32, turned, first)
-        packed[half] = last
-        packed[3 + half] = first
-    both = jnp.where(group < 2, turn(ext[COUNT, 8:16, :], HALO), 0.0)
-    for shift in (32, 64):
-        both = both + turn(both, shift)
-    packed[2] = both
-    packed[5] = both
+        if half == 0:
+            for i in range(4):
+                first = jnp.where(lane == (32 * i + 35) % 128, turn(counts, 31 * i + 35), first)
+        packed[half] = jnp.where(is_spare, spread, last)
+        packed[2 + half] = first
 
 
 def pack_strips(ext, own):
     lane = lanes_of(16)
-    group, place = lane // 32, lane % 32
-
-    def spread(value):
-        return jnp.where(place < 12, turn(value, -12), turn(value, 4))
-
     for field in range(8):
-        for half in range(2):
-            gathered = jnp.zeros((16, 128), jnp.float32)
-            for i in range(4):
-                turned = turn(ext[8 * field + 2 * i + half, 8:24, :], 32 * i + 16)
-                gathered = jnp.where(group == i, turned, gathered)
-            own[2 * field + half] = spread(gathered)
-    gathered = jnp.where(lane < 32, turn(ext[COUNT, 8:24, :], 16), 0.0)
-    for shift in (32, 64):
+        gathered = jnp.zeros((16, 128), jnp.float32)
+        for level in range(LEVELS):
+            gathered = jnp.where(lane // 16 == level, turn(ext[8 * field + level, 8:24, :], 16 * level + 8), gathered)
+        own[field] = gathered
+    gathered = jnp.where(lane < 16, turn(ext[COUNT, 8:24, :], 8), 0.0)
+    for shift in (16, 32, 64):
         gathered = gathered + turn(gathered, shift)
-    own[16] = spread(gathered)
+    own[8] = gathered
+
+
+def run_strip(fields, count):
+    level = (lanes_of(16) // 16).astype(jnp.float32)
+
+    def north_of(value):
+        return pltpu.roll(value, 15, 0)
+
+    def south_of(value):
+        return pltpu.roll(value, 1, 0)
+
+    vel_e, vel_n = fields[6], fields[7]
+    counts = (count, turn(count, -1), turn(count, 1), north_of(count), south_of(count))
+    opened = [jnp.minimum(count, other) > level for other in counts]
+    made = stencil(
+        opened[0],
+        jnp.where(count > level + 1.0, VERT, 0.0),
+        jnp.where(opened[0] & (level > 0.0), VERT, 0.0),
+        vel_e,
+        turn(vel_e, 1),
+        vel_n,
+        south_of(vel_n),
+        *opened[1:],
+    )
+    opens = [jnp.where(opened[which][:8], 0.5, 0.0) for which in (1, 3)]
+
+    def advanced(value, after, before, north, south, names, rows):
+        above, below = turn(value, -16), turn(value, 16)
+        d, e, w, n, s, up, down = (made[name][:rows] for name in names)
+        value, after, before, north, south, above, below = (item[:rows] for item in (value, after, before, north, south, above, below))
+        if names is FORWARD:
+            return (d * value - e * after) + (w * before - n * north) + (s * south + (up * above + down * below))
+        return (d * value + e * after) + (n * north - w * before) + ((up * above + down * below) - s * south)
+
+    fields = list(fields[:6])
+    sums, slopes = {}, {}
+    for step in range(4):
+        for tracer in range(TRACERS):
+            value = fields[tracer]
+            after, north = turn(value, -1), north_of(value)
+            sums[step, tracer] = ((value + after)[:8], (value + north)[:8])
+            if step < 3:
+                fields[tracer] = advanced(value, after, turn(value, 1), north, south_of(value), FORWARD, 16)
+            value = fields[3 + tracer]
+            after, north = turn(value, -1), north_of(value)
+            slopes[step, tracer] = ((after - value)[:8], (north - value)[:8])
+            fields[3 + tracer] = advanced(value, after, turn(value, 1), north, south_of(value), ADJOINT, 16 if step < 3 else 8)
+    grads = []
+    for which in range(2):
+        total = None
+        for step in (1, 2, 0, 3):
+            for tracer in range(TRACERS):
+                term = sums[step, tracer][which] * slopes[3 - step, tracer][which]
+                total = term if total is None else total + term
+        grads.append(total * opens[which])
+    return fields[3:], grads
+
+
+def patch(strip, parts, targets, shift, at_end):
+    states, grads = strip
+    for part, target, base, value in (
+        *((parts[0], targets[0], LEVELS * tracer, value) for tracer, value in enumerate(states)),
+        (parts[1], targets[1], 0, grads[0]),
+        (parts[2], targets[2], 0, grads[1]),
+    ):
+        for level in range(LEVELS):
+            target[base + level] = jnp.where(at_end, turn(value, shift - 16 * level), part[base + level])
+
+
+def eastern_strip(own, east, adj_tracers, adj_east, adj_north):
+    lane = lanes_of(16)
+    place = lane % 16
+    outer = (place >= 8) & (place < 12)
+    odd = lane % 32 >= 16
+    fields = []
+    for field in range(8):
+        arrived = jnp.where(odd, turn(east[1], 20 - 4 * field), turn(east[0], 4 - 4 * field))
+        fields.append(jnp.where(outer, arrived, own[field]))
+    spread = jnp.zeros((16, 128), jnp.float32)
+    for i in range(4):
+        spread = jnp.where(lane == 8 + i, turn(east[0], -27 - 31 * i), spread)
+    for shift in (16, 32, 64):
+        spread = spread + turn(spread, shift)
+    parts = (adj_tracers, adj_east, adj_north)
+    patch(run_strip(fields, jnp.where(outer, spread, own[8])), parts, parts, 120, lanes_of(8) >= 124)
 
 
 def exchange_kernel(
     tracers, cotangent, east_vel, north_vel, sea_mask, level_count,
-    adj_tracers, adj_east, adj_north, own, west, east,
-    ext, packed, mask, count, coefs, opens, states, sums, load_sem, send_sem, recv_sem, answer_sem,
+    adj_tracers, adj_east, adj_north, own_west, west,
+    ext, own, east, packed, mask, count, coefs, opens, states, sums, load_sem, send_sem, recv_sem, answer_sem,
 ):
     loads = []
     for source, target in (
@@ -126,6 +207,7 @@
         loads.append(pltpu.make_async_copy(source, target, load_sem.at[len(loads)]))
         loads[-1].start()
 
+    neighbour = neighbours()
     lat, lats, lon, lons = lax.axis_index("lat"), lax.axis_size("lat"), lax.axis_index("lon"), lax.axis_size("lon")
     exists = {0: lat >= 0, 1: lat < lats - 1, -1: lat > 0}
     barrier = pltpu.get_barrier_semaphore()
@@ -150,17 +232,19 @@
 
         @pl.when(~exists[north])
         def _():
-            west[:, rows, :] = jnp.zeros((3, 4, 128), jnp.float32)
-            east[:, rows, :] = jnp.zeros((3, 4, 128), jnp.float32)
+            west[:, rows, :] = jnp.zeros((2, 4, 128), jnp.float32)
+            east[:, rows, :] = jnp.zeros((2, 4, 128), jnp.float32)
             ext[:, rows.start + 8 : rows.stop + 8, :] = jnp.zeros((PLANES, 4, 128), jnp.float32)
 
+    west[:, 11:13, :] = jnp.zeros((2, 2, 128), jnp.float32)
+    east[:, 11:13, :] = jnp.zeros((2, 2, 128), jnp.float32)
     plan = (
-        (0, 1, packed.at[0:3], west.at[:, 0:8, :]),
-        (1, 1, packed.at[0:3, 4:8, :], west.at[:, 12:16, :]),
-        (-1, 1, packed.at[0:3, 0:4, :], west.at[:, 8:12, :]),
-        (0, -1, packed.at[3:6], east.at[:, 0:8, :]),
-        (1, -1, packed.at[3:6, 4:8, :], east.at[:, 12:16, :]),
-        (-1, -1, packed.at[3:6, 0:4, :], east.at[:, 8:12, :]),
+        (0, 1, packed.at[0:2], west.at[:, 0:8, :]),
+        (1, 1, packed.at[0:2, 5:8, :], west.at[:, 13:16, :]),
+        (-1, 1, packed.at[0:2, 0:3, :], west.at[:, 8:11, :]),
+        (0, -1, packed.at[2:4], east.at[:, 0:8, :]),
+        (1, -1, packed.at[2:4, 5:8, :], east.at[:, 13:16, :]),
+        (-1, -1, packed.at[2:4, 0:3, :], east.at[:, 8:11, :]),
         (1, 0, ext.at[:, 12:16, :], ext.at[:, 20:24, :]),
         (-1, 0, ext.at[:, 8:12, :], ext.at[:, 16:20, :]),
     )
@@ -215,17 +299,18 @@
     wait_recv(along)
     interior(ext, adj_tracers, adj_east, adj_north, coefs, opens, states, sums)
     pack_strips(ext, own)
+    for field in range(STRIPS):
+        own_west[field] = turn(own[field], -4)
     start_answered(~greeted & first)
+    wait_recv(westward)
+    eastern_strip(own, east, adj_tracers, adj_east, adj_north)
     wait_recv(eastward)
-    wait_recv(westward)
     for copy, sent, _ in copies:
         pl.when(sent)(copy.wait_send)
 
 
 def interior(ext, adj_tracers, adj_east, adj_north, coefs, opens, states, sums):
-    margins = jnp.where(inside_grid()[8:16], ext[COUNT, 16:24, :], 0.0)
-    ext[COUNT, 16:24, :] = margins
-    ext[COUNT, 7:8, :] = margins[7:8]
+    ext[COUNT, 7:8, :] = ext[COUNT, 23:24, :]
     ext[COUNT, 24:25, :] = ext[COUNT, 8:9, :]
 
     def each_level(body):
@@ -326,107 +411,22 @@
         each_level(lambda level, step=step: adjoint_step(step, level))
 
 
-def ends_kernel(part_tracers, part_east, part_north, own, west, east, adj_tracers, adj_east, adj_north, rings):
+def western_kernel(part_tracers, part_east, part_north, own, west, adj_tracers, adj_east, adj_north):
     lane = lanes_of(16)
-    place = lane % 32
-    inside = inside_grid()
-
-    def joined(field, half):
-        index = 2 * field + half
-        source = half if field < 8 else 2
-        shift = 4 * field if field < 8 else 0
-        value = jnp.where(place < 4, turn(west[source], -shift), own[index])
-        return jnp.where((place >= 20) & (place < 24), turn(east[source], 16 - shift), value)
-
-    def stored(field, half, value):
-        close_ring(rings, 2 * field + half, value)
-        return value
-
-    count = stored(8, 0, jnp.where(inside, joined(8, 0), 0.0))
-    counts = (count, turn(count, -1), turn(count, 1), rings[16, 9:25, :], rings[16, 7:23, :])
-    least = [jnp.minimum(count, other) for other in counts]
-    made, opens = [], []
+    place = lane % 16
+    outer = place < 4
+    odd = lane % 32 >= 16
+    count = own[8]
     for half in range(2):
-        level = (2 * (lane // 32) + half).astype(jnp.float32)
-        vel_e = joined(6, half)
-        vel_n = stored(7, half, joined(7, half))
-        opened = [value > level for value in least]
-        made.append(
-            stencil(
-                opened[0],
-                jnp.where(count > level + 1.0, VERT, 0.0),
-                jnp.where(opened[0] & (level > 0.0), VERT, 0.0),
-                vel_e,
-                turn(vel_e, 1),
-                vel_n,
-                rings[14 + half, 7:23, :],
-                *opened[1:],
-            )
-        )
-        opens.append([jnp.where(opened[which][:8], 0.5, 0.0) for which in (1, 3)])
-
-    def advanced(field, values, names, rows):
-        near = []
-        for half in range(2):
-            value = values[half]
-            ring = 2 * field + half
-            near.append((value, turn(value, -1), turn(value, 1), rings[ring, 9 : 9 + rows, :], rings[ring, 7 : 7 + rows, :]))
-        results = []
-        for half in range(2):
-            value, after, before, north, south = near[half]
-            d, e, w, n, s, up, down = (made[half][name][:rows] for name in names)
-            above = values[1] if half == 0 else turn(values[0], -32)
-            below = turn(values[1], 32) if half == 0 else values[0]
-            if names is FORWARD:
-                result = d * value - e * after + w * before - n * north + s * south
-            else:
-                result = d * value + e * after - w * before + n * north - s * south
-            results.append(result + up * above + down * below)
-        return results, near
-
-    fields = [[stored(field, half, joined(field, half)) for half in range(2)] for field in range(6)]
-    sums = []
-    for step in range(4):
-        sums.append([])
-        for tracer in range(TRACERS):
-            if step < 3:
-                results, near = advanced(tracer, fields[tracer], FORWARD, 16)
-            else:
-                results = fields[tracer]
-                near = [(value, turn(value, -1), None, rings[2 * tracer + half, 9:25, :]) for half, value in enumerate(results)]
-            sums[step].append([(value[:8] + after[:8], value[:8] + north[:8]) for value, after, _, north, *_ in near])
-            if step < 3:
-                fields[tracer] = [stored(tracer, half, value) for half, value in enumerate(results)]
-    grads = [[jnp.zeros((8, 128), jnp.float32)] * 2 for half in range(2)]
-    for step in range(4):
-        for tracer in range(TRACERS):
-            rows = 16 if step < 3 else 8
-            values = [value[:rows] for value in fields[3 + tracer]]
-            results, near = advanced(3 + tracer, values, ADJOINT, rows)
-            for half in range(2):
-                value, after, _, north, _ = near[half]
-                east_sum, north_sum = sums[3 - step][tracer][half]
-                grads[half] = [
-                    grads[half][0] + east_sum * (after[:8] - value[:8]),
-                    grads[half][1] + north_sum * (north[:8] - value[:8]),
-                ]
-            fields[3 + tracer] = [stored(3 + tracer, half, value) if step < 3 else value for half, value in enumerate(results)]
-
-    short = lanes_of(8)
-    at_end = (short < 4) | (short >= 124)
-    short_place = short % 32
-
-    def patched(value, part, target, half, base):
-        value = jnp.where(short_place < 4, turn(value, -16), value)
-        for i in range(4):
-            slab = base + 2 * i + half
-            target[slab] = jnp.where(at_end, turn(value, -(32 * i + 4)), part[slab])
-
-    for half in range(2):
-        for tracer in range(TRACERS):
-            patched(fields[3 + tracer][half], part_tracers, adj_tracers, half, LEVELS * tracer)
-        patched(grads[half][0] * opens[half][0], part_east, adj_east, half, 0)
-        patched(grads[half][1] * opens[half][1], part_north, adj_north, half, 0)
+        for column, field in enumerate(SPARE):
+            here = (place == column) & (odd if half else ~odd)
+            count = jnp.where(here, turn(west[half], 16 * half + column - HALO * field), count)
+    fields = []
+    for field in range(8):
+        arrived = jnp.where(odd, turn(west[1], 16 - HALO * field), turn(west[0], -HALO * field))
+        fields.append(jnp.where(outer, arrived, own[field]))
+    parts, targets = (part_tracers, part_east, part_north), (adj_tracers, adj_east, adj_north)
+    patch(run_strip(fields, count), parts, targets, -4, lanes_of(8) < 4)
 
 
 def on_device(tracers, cotangent, east_vel, north_vel, sea_mask, level_count):
@@ -444,14 +444,15 @@
         out_shape=(
             *results,
             jax.ShapeDtypeStruct((STRIPS, 16, 128), f32),
-            jax.ShapeDtypeStruct((3, 16, 128), f32),
-            jax.ShapeDtypeStruct((3, 16, 128), f32),
+            jax.ShapeDtypeStruct((2, 16, 128), f32),
         ),
         in_specs=[pl.BlockSpec(memory_space=pltpu.HBM)] * 6,
-        out_specs=(vmem,) * 6,
+        out_specs=(vmem,) * 5,
         scratch_shapes=[
             pltpu.VMEM((PLANES, ROWS, 128), f32),
-            pltpu.VMEM((6, 8, 128), f32),
+            pltpu.VMEM((STRIPS, 16, 128), f32),
+            pltpu.VMEM((2, 16, 128), f32),
+            pltpu.VMEM((4, 8, 128), f32),
             pltpu.VMEM((8, 128), jnp.int32),
             pltpu.VMEM((8, 128), jnp.int32),
             pltpu.VMEM((LEVELS, 11, 16, 128), f32),
@@ -466,12 +467,11 @@
         compiler_params=pltpu.CompilerParams(collective_id=0, has_side_effects=True, vmem_limit_bytes=16 << 20),
     )(*(pltpu.with_memory_space_constraint(operand, pltpu.HBM) for operand in operands))
     adj_tracers, adj_east, adj_north = pl.pallas_call(
-        ends_kernel,
-        name="ends",
+        western_kernel,
+        name="western",
         out_shape=results,
-        in_specs=[vmem] * 6,
+        in_specs=[vmem] * 5,
         out_specs=(vmem,) * 3,
-        scratch_shapes=[pltpu.VMEM((STRIPS, ROWS, 128), f32)],
         compiler_params=pltpu.CompilerParams(vmem_limit_bytes=16 << 20),
     )(*parts)
     return adj_tracers.reshape(tracers.shape), adj_east, adj_north

time: 25 us -> 24.8 us (level)
  no operation moved by 1% of the time
where the time goes in v3:
time: 24.8 us; the launch traced here: 24.6 us
  Pallas kernels  24 us (97%)
  between operations  0.64 us (3%)
    pallas_call x1, Pallas kernels, on_device(): pl.pallas_call(exchange_kernel, name='exchange', out_shape=(*results, jax...  22.8 us
    pallas_call x1, Pallas kernels, on_device(): pl.pallas_call(western_kernel, name='western', out_shape=results, in_spec...  1.21 us

profile of v3, /device:TPU:1, one launch (start us, length us, event | category | flops | bytes accessed | tf_op | source)
XLA Modules:
  0.0 24.6 jit_solution(14977209325419192613)
XLA Ops:
  0.6 22.8 %exchange.1 = (f32[24,8,128]{2,1,0:T(8,128)S(1)}, f32[8,8,128]{2,1,0:T(8,128)S(1)}, f32[8,8,128]{2,1,0:T(8,128)S(1)}, f32[9,16,128]{2,1,0:T(8,128)S(1)}, f32[2,16,128]{2,1,0:T(8,128)S(1)}) custom-call(f32[24,8,128]{2,1,0:T(8,128)} %bitcast.3, f32[24,8,128]{2,1,0:T(8,128)} %bitcast.4, f32[8,8,128]{2,1,0:T(8,128)} %east_vel.1, f32[8,8,128]{2,1,0:T(8,128)} %north_vel.1, ...), custom_call_target="tpu_custom_call" | custom-call | tf_op jit(solution)/shard_map/exchange/pallas_call | solution.py:441
  23.4 1.2 %western.1 = (f32[24,8,128]{2,1,0:T(8,128)}, f32[8,8,128]{2,1,0:T(8,128)}, f32[8,8,128]{2,1,0:T(8,128)}) custom-call(f32[24,8,128]{2,1,0:T(8,128)S(1)} %get-tuple-element.11.part_tracers, f32[8,8,128]{2,1,0:T(8,128)S(1)} %get-tuple-element.12.part_east, f32[8,8,128]{2,1,0:T(8,128)S(1)} %get-tuple-element.13.part_north, ...), custom_call_target="tpu_custom_call" | custom-call | tf_op jit(solution)/shard_map/western/pallas_call | solution.py:469

commit v4 on v3

--- a/solution.py
+++ b/solution.py
@@ -45,7 +45,7 @@
     pw, qw = open_pair(open_west, vel_west)
     pn, qn = open_pair(open_north, vel_north)
     ps, qs = open_pair(open_south, vel_south)
-    diagonal = jnp.where(wet, 1.0, 0.0) - pe + qw - pn + qs - up - down
+    diagonal = (jnp.where(wet, 1.0, 0.0) - (up + down)) + ((qw - pe) + (qs - pn))
     return diagonal, pe, pw, qe, qw, pn, ps, qn, qs, up, down
 
 
@@ -66,7 +66,7 @@
     return place >= 0, (place != places - 1) & (place != 0)
 
 
-def pack_ends(ext, packed):
+def pack_last(ext, packed):
     lane = lanes_of(8)
     group = lane // HALO
     counts = ext[COUNT, 8:16, :]
@@ -78,17 +78,26 @@
     is_spare = (lane % 32 == 0) | (lane % 32 == 4) | (lane % 32 == 8) | (lane % 32 == 28)
     for half in range(2):
         last = jnp.zeros((8, 128), jnp.float32)
+        for field in range(8):
+            for i in range(4):
+                place = 8 * i + field
+                last = jnp.where(group == place, turn(ext[8 * field + 2 * i + half, 8:16, :], HALO * (place + 1)), last)
+        packed[half] = jnp.where(is_spare, spread, last)
+
+
+def pack_first(ext, packed):
+    lane = lanes_of(8)
+    group = lane // HALO
+    counts = ext[COUNT, 8:16, :]
+    for half in range(2):
         first = jnp.zeros((8, 128), jnp.float32)
         for field in range(8):
             for i in range(4):
                 place = 8 * i + field
-                turned = turn(ext[8 * field + 2 * i + half, 8:16, :], HALO * (place + 1))
-                last = jnp.where(group == place, turned, last)
-                first = jnp.where(group == (place + 1) % 32, turned, first)
+                first = jnp.where(group == (place + 1) % 32, turn(ext[8 * field + 2 * i + half, 8:16, :], HALO * (place + 1)), first)
         if half == 0:
             for i in range(4):
                 first = jnp.where(lane == (32 * i + 35) % 128, turn(counts, 31 * i + 35), first)
-        packed[half] = jnp.where(is_spare, spread, last)
         packed[2 + half] = first
 
 
@@ -154,9 +163,9 @@
     for which in range(2):
         total = None
         for step in (1, 2, 0, 3):
-            for tracer in range(TRACERS):
-                term = sums[step, tracer][which] * slopes[3 - step, tracer][which]
-                total = term if total is None else total + term
+            terms = [sums[step, tracer][which] * slopes[3 - step, tracer][which] for tracer in range(TRACERS)]
+            part = (terms[0] + terms[1]) + terms[2]
+            total = part if total is None else total + part
         grads.append(total * opens[which])
     return fields[3:], grads
 
@@ -197,8 +206,8 @@
 ):
     loads = []
     for source, target in (
-        (tracers, ext.at[TRACER : TRACER + 24, 8:16, :]),
-        (cotangent, ext.at[COTAN : COTAN + 24, 8:16, :]),
+        *((tracers.at[at : at + 8], ext.at[TRACER + at : TRACER + at + 8, 8:16, :]) for at in (0, 8, 16)),
+        *((cotangent.at[at : at + 8], ext.at[COTAN + at : COTAN + at + 8, 8:16, :]) for at in (0, 8, 16)),
         (east_vel, ext.at[EAST : EAST + 8, 8:16, :]),
         (north_vel, ext.at[NORTH : NORTH + 8, 8:16, :]),
         (sea_mask, mask),
@@ -239,8 +248,8 @@
     west[:, 11:13, :] = jnp.zeros((2, 2, 128), jnp.float32)
     east[:, 11:13, :] = jnp.zeros((2, 2, 128), jnp.float32)
     plan = (
+        (1, 1, packed.at[0:2, 5:8, :], west.at[:, 13:16, :]),
         (0, 1, packed.at[0:2], west.at[:, 0:8, :]),
-        (1, 1, packed.at[0:2, 5:8, :], west.at[:, 13:16, :]),
         (-1, 1, packed.at[0:2, 0:3, :], west.at[:, 8:11, :]),
         (0, -1, packed.at[2:4], east.at[:, 0:8, :]),
         (1, -1, packed.at[2:4, 5:8, :], east.at[:, 13:16, :]),
@@ -282,8 +291,9 @@
     for load in loads:
         load.wait()
     ext[COUNT, 8:16, :] = jnp.where(mask[...] == 1, count[...], 0).astype(jnp.float32)
-    pack_ends(ext, packed)
+    pack_last(ext, packed)
     start(eastward, lon >= 0)
+    pack_first(ext, packed)
     greeted = greetings(-1)[1]
     start(westward, greeted)
     start(along, lon >= 0)
@@ -301,12 +311,12 @@
     pack_strips(ext, own)
     for field in range(STRIPS):
         own_west[field] = turn(own[field], -4)
-    start_answered(~greeted & first)
     wait_recv(westward)
     eastern_strip(own, east, adj_tracers, adj_east, adj_north)
-    wait_recv(eastward)
+    start_answered(~greeted & first)
     for copy, sent, _ in copies:
         pl.when(sent)(copy.wait_send)
+    wait_recv(eastward)
 
 
 def interior(ext, adj_tracers, adj_east, adj_north, coefs, opens, states, sums):
@@ -459,7 +469,7 @@
             pltpu.VMEM((LEVELS, 2, 8, 128), f32),
             pltpu.VMEM((72, ROWS, 128), f32),
             pltpu.VMEM((4, 2, 24, 8, 128), f32),
-            pltpu.SemaphoreType.DMA((6,)),
+            pltpu.SemaphoreType.DMA((10,)),
             pltpu.SemaphoreType.DMA((8,)),
             pltpu.SemaphoreType.DMA((8,)),
             pltpu.SemaphoreType.REGULAR((1,)),

time: 24.8 us -> 24.4 us (0.984)
  Pallas kernels: 24 us -> 23.6 us
    pallas_call x1, Pallas kernels: 22.8 us -> 22.4 us  [on_device(): pl.pallas_call(exchange_kernel, name='exchange', out_shape=(*results, jax...]
where the time goes in v4:
time: 24.4 us; the launch traced here: 24.2 us
  Pallas kernels  23.6 us (97%)
  between operations  0.64 us (3%)
    pallas_call x1, Pallas kernels, on_device(): pl.pallas_call(exchange_kernel, name='exchange', out_shape=(*results, jax...  22.4 us
    pallas_call x1, Pallas kernels, on_device(): pl.pallas_call(western_kernel, name='western', out_shape=results, in_spec...  1.21 us

profile of v4, /device:TPU:1, one launch (start us, length us, event | category | flops | bytes accessed | tf_op | source)
XLA Modules:
  0.0 24.2 jit_solution(4828090014237343691)
XLA Ops:
  0.6 22.4 %exchange.1 = (f32[24,8,128]{2,1,0:T(8,128)S(1)}, f32[8,8,128]{2,1,0:T(8,128)S(1)}, f32[8,8,128]{2,1,0:T(8,128)S(1)}, f32[9,16,128]{2,1,0:T(8,128)S(1)}, f32[2,16,128]{2,1,0:T(8,128)S(1)}) custom-call(f32[24,8,128]{2,1,0:T(8,128)} %bitcast.3, f32[24,8,128]{2,1,0:T(8,128)} %bitcast.4, f32[8,8,128]{2,1,0:T(8,128)} %east_vel.1, f32[8,8,128]{2,1,0:T(8,128)} %north_vel.1, ...), custom_call_target="tpu_custom_call" | custom-call | tf_op jit(solution)/shard_map/exchange/pallas_call | solution.py:451
  23.0 1.2 %western.1 = (f32[24,8,128]{2,1,0:T(8,128)}, f32[8,8,128]{2,1,0:T(8,128)}, f32[8,8,128]{2,1,0:T(8,128)}) custom-call(f32[24,8,128]{2,1,0:T(8,128)S(1)} %get-tuple-element.11.part_tracers, f32[8,8,128]{2,1,0:T(8,128)S(1)} %get-tuple-element.12.part_east, f32[8,8,128]{2,1,0:T(8,128)S(1)} %get-tuple-element.13.part_north, ...), custom_call_target="tpu_custom_call" | custom-call | tf_op jit(solution)/shard_map/western/pallas_call | solution.py:479

commit v5 on v4

--- a/solution.py
+++ b/solution.py
@@ -286,13 +286,13 @@
 
     eastward, westward, along = copies[0:3], copies[3:6], copies[6:8]
     first, last = lon == 0, lon == lons - 1
-    pl.semaphore_wait(barrier, expected)
-    answer(1, answer_sem.at[0])
     for load in loads:
         load.wait()
     ext[COUNT, 8:16, :] = jnp.where(mask[...] == 1, count[...], 0).astype(jnp.float32)
     pack_last(ext, packed)
+    pl.semaphore_wait(barrier, expected)
     start(eastward, lon >= 0)
+    answer(1, answer_sem.at[0])
     pack_first(ext, packed)
     greeted = greetings(-1)[1]
     start(westward, greeted)

time: 24.4 us -> 24.4 us (level)
  no operation moved by 1% of the time
where the time goes in v5:
time: 24.4 us; the launch traced here: 24.2 us
  Pallas kernels  23.6 us (97%)
  between operations  0.64 us (3%)
    pallas_call x1, Pallas kernels, on_device(): pl.pallas_call(exchange_kernel, name='exchange', out_shape=(*results, jax...  22.4 us
    pallas_call x1, Pallas kernels, on_device(): pl.pallas_call(western_kernel, name='western', out_shape=results, in_spec...  1.21 us

profile of v5, /device:TPU:1, one launch (start us, length us, event | category | flops | bytes accessed | tf_op | source)
XLA Modules:
  0.0 24.2 jit_solution(10138678434558407555)
XLA Ops:
  0.6 22.4 %exchange.1 = (f32[24,8,128]{2,1,0:T(8,128)S(1)}, f32[8,8,128]{2,1,0:T(8,128)S(1)}, f32[8,8,128]{2,1,0:T(8,128)S(1)}, f32[9,16,128]{2,1,0:T(8,128)S(1)}, f32[2,16,128]{2,1,0:T(8,128)S(1)}) custom-call(f32[24,8,128]{2,1,0:T(8,128)} %bitcast.3, f32[24,8,128]{2,1,0:T(8,128)} %bitcast.4, f32[8,8,128]{2,1,0:T(8,128)} %east_vel.1, f32[8,8,128]{2,1,0:T(8,128)} %north_vel.1, ...), custom_call_target="tpu_custom_call" | custom-call | tf_op jit(solution)/shard_map/exchange/pallas_call | solution.py:451
  23.0 1.2 %western.1 = (f32[24,8,128]{2,1,0:T(8,128)}, f32[8,8,128]{2,1,0:T(8,128)}, f32[8,8,128]{2,1,0:T(8,128)}) custom-call(f32[24,8,128]{2,1,0:T(8,128)S(1)} %get-tuple-element.11.part_tracers, f32[8,8,128]{2,1,0:T(8,128)S(1)} %get-tuple-element.12.part_east, f32[8,8,128]{2,1,0:T(8,128)S(1)} %get-tuple-element.13.part_north, ...), custom_call_target="tpu_custom_call" | custom-call | tf_op jit(solution)/shard_map/western/pallas_call | solution.py:479

commit v6 on v4

--- a/solution.py
+++ b/solution.py
@@ -202,7 +202,7 @@
 def exchange_kernel(
     tracers, cotangent, east_vel, north_vel, sea_mask, level_count,
     adj_tracers, adj_east, adj_north, own_west, west,
-    ext, own, east, packed, mask, count, coefs, opens, states, sums, load_sem, send_sem, recv_sem, answer_sem,
+    ext, own, east, packed, mask, count, coefs, opens, states, sums, load_sem, send_sem, recv_sem, answer_sem, told_sem,
 ):
     loads = []
     for source, target in (
@@ -221,7 +221,8 @@
     exists = {0: lat >= 0, 1: lat < lats - 1, -1: lat > 0}
     barrier = pltpu.get_barrier_semaphore()
     in_column = jnp.where(exists[1], 1, 0) + jnp.where(exists[-1], 1, 0)
-    expected = in_column
+    first, last = (lon == 0) & (lons > 2), (lon == lons - 1) & (lons > 2)
+    expected = jnp.where(last, 0, in_column)
     for side in (-1, 1):
         greets, greeted = greetings(side)
         expected = expected + jnp.where(greeted, in_column + 1, 0)
@@ -233,7 +234,7 @@
 
     for north in (1, -1):
 
-        @pl.when(exists[north])
+        @pl.when(exists[north] & ~last)
         def _():
             pl.semaphore_signal(barrier, inc=1, device_id=neighbour(north, 0), device_id_type=MESH)
 
@@ -285,7 +286,6 @@
                 pl.semaphore_signal(theirs, inc=1, device_id=neighbour(north, side), device_id_type=MESH)
 
     eastward, westward, along = copies[0:3], copies[3:6], copies[6:8]
-    first, last = lon == 0, lon == lons - 1
     pl.semaphore_wait(barrier, expected)
     answer(1, answer_sem.at[0])
     for load in loads:
@@ -296,15 +296,24 @@
     pack_first(ext, packed)
     greeted = greetings(-1)[1]
     start(westward, greeted)
-    start(along, lon >= 0)
+    start(along, ~last)
 
     def start_answered(condition):
         @pl.when(condition)
         def _():
             pl.semaphore_wait(answer_sem.at[0], in_column + 1)
 
+        @pl.when(condition & first)
+        def _():
+            pl.semaphore_signal(told_sem, inc=1, device_id=neighbour(0, -1), device_id_type=MESH)
+
         start(westward, condition)
 
+    @pl.when(last)
+    def _():
+        pl.semaphore_wait(told_sem, 1)
+
+    start(along, last)
     start_answered(~greeted & last)
     wait_recv(along)
     interior(ext, adj_tracers, adj_east, adj_north, coefs, opens, states, sums)
@@ -473,6 +482,7 @@
             pltpu.SemaphoreType.DMA((8,)),
             pltpu.SemaphoreType.DMA((8,)),
             pltpu.SemaphoreType.REGULAR((1,)),
+            pltpu.SemaphoreType.REGULAR,
         ],
         compiler_params=pltpu.CompilerParams(collective_id=0, has_side_effects=True, vmem_limit_bytes=16 << 20),
     )(*(pltpu.with_memory_space_constraint(operand, pltpu.HBM) for operand in operands))

time: 24.4 us -> 24.4 us (level)
  no operation moved by 1% of the time
where the time goes in v6:
time: 24.4 us; the launch traced here: 24.2 us
  Pallas kernels  23.6 us (97%)
  between operations  0.64 us (3%)
    pallas_call x1, Pallas kernels, on_device(): pl.pallas_call(exchange_kernel, name='exchange', out_shape=(*results, jax...  22.4 us
    pallas_call x1, Pallas kernels, on_device(): pl.pallas_call(western_kernel, name='western', out_shape=results, in_spec...  1.21 us

profile of v6, /device:TPU:1, one launch (start us, length us, event | category | flops | bytes accessed | tf_op | source)
XLA Modules:
  0.0 24.2 jit_solution(15062958133187694252)
XLA Ops:
  0.6 22.4 %exchange.1 = (f32[24,8,128]{2,1,0:T(8,128)S(1)}, f32[8,8,128]{2,1,0:T(8,128)S(1)}, f32[8,8,128]{2,1,0:T(8,128)S(1)}, f32[9,16,128]{2,1,0:T(8,128)S(1)}, f32[2,16,128]{2,1,0:T(8,128)S(1)}) custom-call(f32[24,8,128]{2,1,0:T(8,128)} %bitcast.3, f32[24,8,128]{2,1,0:T(8,128)} %bitcast.4, f32[8,8,128]{2,1,0:T(8,128)} %east_vel.1, f32[8,8,128]{2,1,0:T(8,128)} %north_vel.1, ...), custom_call_target="tpu_custom_call" | custom-call | tf_op jit(solution)/shard_map/exchange/pallas_call | solution.py:460
  23.0 1.2 %western.1 = (f32[24,8,128]{2,1,0:T(8,128)}, f32[8,8,128]{2,1,0:T(8,128)}, f32[8,8,128]{2,1,0:T(8,128)}) custom-call(f32[24,8,128]{2,1,0:T(8,128)S(1)} %get-tuple-element.11.part_tracers, f32[8,8,128]{2,1,0:T(8,128)S(1)} %get-tuple-element.12.part_east, f32[8,8,128]{2,1,0:T(8,128)S(1)} %get-tuple-element.13.part_north, ...), custom_call_target="tpu_custom_call" | custom-call | tf_op jit(solution)/shard_map/western/pallas_call | solution.py:489
